TPU v7x, 256 devices: a whole 4x4x8 slice. The times are simulated.
256 devices in a mesh: seq: 64 (over z, x, y_lo), head: 4 (over y_hi, core).
Axes of the slice: x: 4, y: 4 (y_hi: 2, y_lo: 2; y = y_hi * 2 + y_lo), z: 8, core: 2. Of those that a mesh axis runs over, the one named last changes fastest.
Arguments:
- queries: bfloat16 [512, 64, 128], P('seq', 'head'), may hold values from -6 to 6
- shared_key_rows: bfloat16 [32768, 8, 128], P('seq', 'head'), may hold values from -10 to 10
- shared_value_rows: bfloat16 [32768, 8, 128], P('seq', 'head'), may hold values from -6 to 6
- tenant_key_rows: bfloat16 [262144, 8, 128], P('seq', 'head'), may hold values from -10 to 10
- tenant_value_rows: bfloat16 [262144, 8, 128], P('seq', 'head'), may hold values from -6 to 6
- tenant_ids: int32 [512], replicated, may hold values from 0 to 15, as said below
- tenant_len: int32 [16], replicated, may hold values from 4096 to 16384, as said below
- priv_len: int32 [512], P('seq'), may hold values from 0 to 1024, as said below
- page_table: int32 [512, 8], P('seq'), may hold values from 0 to 35, as said below
- private_key_pages: bfloat16 [2304, 128, 8, 128], P('seq', None, 'head'), may hold values from -12 to 12
- private_value_pages: bfloat16 [2304, 128, 8, 128], P('seq', None, 'head'), may hold values from -6 to 6
- out_weight: bfloat16 [8192, 8192], P('head', 'seq'), may hold values from -0.0625 to 0.0625
Outputs:
- attended_out: bfloat16 [512, 8192], P('head', 'seq')
Inputs may be any that keep to these rules, and one draw needn't show every extreme that they name: `tenant_ids`: each tenant has at most 48 requests, and some tenant exactly 48. `tenant_len`: some tenant's prefix has exactly 16384 positions. `priv_len`: in each owner's block of 8 requests one has exactly 1024 private positions, and the block's requests together live on at most 36 pages. `page_table`: entries index the owner's own pool; the pages that hold live positions of an owner's requests are all different.
All inputs are finite; a program needn't handle non-finite values.
Results may differ from a plain program's by a relative error of at most 0.005.
Values may be sent and summed in bfloat16 or wider, within the bound.
A program may use at most 128 MiB of HBM per device.

v0:
```python
import math

import jax
import jax.numpy as jnp
from jax import lax
from jax.sharding import PartitionSpec as P

score_masked = -1e30


def finish(scores, value_rows, usable, form):
    if usable is not None:
        scores = jnp.where(usable, scores, score_masked)
    maxima = jnp.max(scores, axis=-1)
    weights = jnp.exp(scores - maxima[..., None])
    if usable is not None:
        weights = jnp.where(usable, weights, 0.0)
    totals = jnp.sum(weights, axis=-1)
    rounded = weights.astype(jnp.bfloat16)
    outputs = jnp.einsum(form, rounded, value_rows, preferred_element_type=jnp.float32)
    return (maxima, totals, outputs)


def combine(earlier, later):
    highest = jnp.maximum(earlier[0], later[0])
    early_weight = jnp.exp(earlier[0] - highest)
    late_weight = jnp.exp(later[0] - highest)
    return (
        highest,
        early_weight * earlier[1] + late_weight * later[1],
        early_weight[..., None] * earlier[2] + late_weight[..., None] * later[2],
    )


def local(
    queries,
    shared_key_rows,
    shared_value_rows,
    tenant_key_rows,
    tenant_value_rows,
    tenant_ids,
    tenant_len,
    priv_len,
    page_table,
    private_key_pages,
    private_value_pages,
    out_weight,
):
    owned_rows, local_heads, head_dim = queries.shape
    kv_local = shared_key_rows.shape[1]
    group_query_count = local_heads // kv_local
    factor = 1.0 / math.sqrt(head_dim)
    seq_count = lax.axis_size("seq")
    requests = owned_rows * seq_count
    everyone = lax.all_gather(queries, "seq", axis=0, tiled=True)
    group_rows = everyone.reshape(requests, kv_local, group_query_count, head_dim)
    scores = (
        jnp.einsum(
            "rkgd,tkd->rkgt", group_rows, shared_key_rows, preferred_element_type=jnp.float32
        )
        * factor
    )
    shared_parts = finish(scores, shared_value_rows, None, "rkgt,tkd->rkgd")
    position = lax.axis_index("seq")
    tenant = position // 4
    quarter = position % 4
    capacity = 6 * owned_rows
    chosen = jnp.nonzero(tenant_ids == tenant, size=capacity, fill_value=requests)[0]
    picked = jnp.minimum(chosen, requests - 1)
    extent = tenant_key_rows.shape[0]
    tenant_scores = (
        jnp.einsum(
            "rkgd,tkd->rkgt",
            group_rows[picked],
            tenant_key_rows,
            preferred_element_type=jnp.float32,
        )
        * factor
    )
    extent_left = tenant_len[tenant] - quarter * extent
    usable = (jnp.arange(extent, dtype=jnp.int32) < extent_left)[None, None, None, :]
    tenant_parts = finish(tenant_scores, tenant_value_rows, usable, "rkgt,tkd->rkgd")
    current = tuple((whole[picked] for whole in shared_parts))
    merged = combine(current, tenant_parts)
    joined = tuple(
        (whole.at[chosen].set(update, mode="drop") for whole, update in zip(shared_parts, merged))
    )
    arrivals = [lax.all_to_all(joined, "seq", split_axis=0, concat_axis=0, tiled=True)]
    local_queries = queries.reshape(owned_rows, kv_local, group_query_count, head_dim)
    paged_key_rows = private_key_pages[page_table].reshape(owned_rows, -1, kv_local, head_dim)
    paged_value_rows = private_value_pages[page_table].reshape(owned_rows, -1, kv_local, head_dim)
    private_scores = (
        jnp.einsum(
            "rkgd,rtkd->rkgt", local_queries, paged_key_rows, preferred_element_type=jnp.float32
        )
        * factor
    )
    private_usable = (
        jnp.arange(paged_key_rows.shape[1], dtype=jnp.int32)[None, :] < priv_len[:, None]
    )[:, None, None, :]
    private_pieces = finish(private_scores, paged_value_rows, private_usable, "rkgt,rtkd->rkgd")
    small_shape = (seq_count, owned_rows, kv_local, group_query_count)
    maxima = jnp.concatenate(
        [piece[0].reshape(small_shape) for piece in arrivals] + [private_pieces[0][None]], axis=0
    )
    totals = jnp.concatenate(
        [piece[1].reshape(small_shape) for piece in arrivals] + [private_pieces[1][None]], axis=0
    )
    outputs = jnp.concatenate(
        [piece[2].reshape(small_shape + (head_dim,)) for piece in arrivals]
        + [private_pieces[2][None]],
        axis=0,
    )
    highest = jnp.max(maxima, axis=0)
    scaling = jnp.exp(maxima - highest[None])
    denominator = jnp.sum(scaling * totals, axis=0)
    numerator = jnp.sum(scaling[..., None] * outputs, axis=0)
    attended = (
        (numerator / denominator[..., None])
        .astype(jnp.bfloat16)
        .reshape(owned_rows, local_heads * head_dim)
    )
    partial_out = jnp.dot(
        lax.all_gather(attended, "seq", axis=0, tiled=True),
        out_weight,
        preferred_element_type=jnp.float32,
    )
    summed = lax.psum_scatter(partial_out, "head", scatter_dimension=0, tiled=True)
    return summed.astype(jnp.bfloat16)


def solution(mesh):
    placed = (
        P("seq", "head", None),
        P("seq", "head", None),
        P("seq", "head", None),
        P("seq", "head", None),
        P("seq", "head", None),
        P(),
        P(),
        P("seq"),
        P("seq", None),
        P("seq", None, "head", None),
        P("seq", None, "head", None),
        P("head", "seq"),
    )
    return jax.shard_map(
        local, mesh=mesh, in_specs=placed, out_specs=P("head", "seq"), check_vma=False
    )
```

profile of v0, /device:TPU:1, one launch (start us, length us, event | category | flops | bytes accessed | tf_op | source)
XLA Modules:
  0.0 828.5 jit_solution(8067424946137802625)
XLA Ops:
  6.5 0.7 all-gather.3.cloned.1.call-update
  7.3 1.3 convert_reduce_fusion
  9.2 4.1 scatter_custom_fusion
  13.5 1.2 dynamic_slice.3
  15.4 1.3 fusion.70
  16.7 250.8 %all-gather.3.cloned.1.call-done = bf16[512,16,128]{2,1,0:T(8,128)(2,1)} async-done(((bf16[8,16,128]{2,1,0:T(8,128)(2,1)}), bf16[512,16,128]{2,1,0:T(8,128)(2,1)}) %all-gather.3.cloned.1.call-update) | async-done | bytes 2097168 | tf_op jit(solution)/shard_map/all_gather | solution.py:55
  267.5 2.2 gather_fusion.1
  269.7 8.2 bitcast_reduce_fusion.1
  277.9 6.8 fusion.5
  284.8 0.7 copy.126
  285.4 2.1 copy.94
  287.6 8.1 bitcast_reduce_fusion
  295.9 8.6 %fusion.1 = f32[512,2,8]{0,2,1:T(8,128)S(1)} fusion(f32[2,512,512,8]{2,1,3,0:T(8,128)} %get-tuple-element.18, f32[512,2,8]{0,2,1:T(8,128)S(1)} %get-tuple-element.17), kind=kLoop, calls=%fused_computation.13 | loop fusion | flops 12574720 | bytes 16842752 | tf_op jit(solution)/shard_map/reduce_sum | solution.py:18
  305.1 0.7 copy.101
  306.0 0.6 gather_fusion.5
  306.6 0.7 copy.125
  307.3 1.3 multiply_add_fusion
  308.6 0.8 copy.128
  309.4 2.1 scatter_fusion.2
  311.6 1.4 reshape.312
  313.0 14.2 %all-to-all-start.2 = ((f32[64,1,128]{2,1,0:T(1,128)}), f32[64,1,128]{2,1,0:T(1,128)S(1)}, u32[]{:S(2)}, u32[]{:S(2)}) async-start(f32[64,1,128]{2,1,0:T(1,128)} %reshape.312), calls=%async_computation.2 | async-start | bytes 65536 | tf_op jit(solution)/shard_map/all_to_all | solution.py:88
  327.2 11.9 %fusion.20 = f32[512,2,8,128]{3,0,2,1:T(8,128)} fusion(f32[2,512,512,8]{2,1,3,0:T(8,128)} %get-tuple-element.18, f32[512,2,8]{0,2,1:T(8,128)S(1)} %get-tuple-element.17, bf16[512,2,128,1]{2,1,0,3:T(2,128)(2,1)} %bitcast.87), kind=kOutput, calls=%fused_computation.34 | convolution fusion | flops 1086324736 | bytes 21266432 | tf_op jit(solution)/shard_map/rkgt,tkd->rkgd/dot_general | solution.py:20
  339.1 6.6 copy.121
  345.8 3.5 gather_fusion.3
  349.6 2.0 scatter_fusion
  351.6 1.4 reshape.310
  353.0 10.7 %all-to-all-start = ((f32[64,1,128]{2,1,0:T(1,128)}), f32[64,1,128]{2,1,0:T(1,128)S(1)}, u32[]{:S(2)}, u32[]{:S(2)}) async-start(f32[64,1,128]{2,1,0:T(1,128)} %reshape.310), calls=%async_computation | async-start | bytes 65536 | tf_op jit(solution)/shard_map/all_to_all | solution.py:88
  363.6 7.7 fusion.39
  371.4 5.5 scatter_fusion.1
  376.9 10.7 %all-to-all-start.1 = ((f32[512,2,8,128]{3,2,1,0:T(8,128)}), f32[512,2,8,128]{3,2,1,0:T(8,128)}, u32[]{:S(2)}, u32[]{:S(2)}) async-start(f32[512,2,8,128]{3,2,1,0:T(8,128)} %scatter_fusion.1), calls=%async_computation.1 | async-start | bytes 8388608 | tf_op jit(solution)/shard_map/all_to_all | solution.py:88
  388.0 10.7 %gather_fusion.4 = bf16[64,128,2,128]{3,2,1,0:T(2,128)(2,1)} fusion(bf16[36,128,2,128]{3,2,1,0:T(2,128)(2,1)S(1)} %copy-done, s32[1024]{0:T(1024)S(1)} %pad_clamp_fusion), kind=kCustom, calls=%fused_computation.4 | custom fusion | bytes 8388864 | tf_op jit(solution)/shard_map/gather | solution.py:91
  398.6 12.4 %gather_fusion.2 = bf16[64,128,2,128]{3,2,1,0:T(2,128)(2,1)} fusion(bf16[36,128,2,128]{3,2,1,0:T(2,128)(2,1)} %param.21, s32[1024]{0:T(1024)S(1)} %pad_clamp_fusion), kind=kCustom, calls=%fused_computation.2 | custom fusion | bytes 8388864 | tf_op jit(solution)/shard_map/gather | solution.py:90
  411.1 3.5 fusion.79
  414.8 0.8 copy.132
  415.6 0.8 copy.109
  416.4 3.6 fusion.50
  420.5 0.7 reduce.9
  421.2 0.8 reshape.311
  422.7 0.7 reduce.8
  423.4 0.8 reshape.313
  424.6 2.2 fusion.64
  426.8 1.3 copy.111
  428.1 10.7 %all-to-all-done.1 = f32[512,2,8,128]{3,2,1,0:T(8,128)} async-done(((f32[512,2,8,128]{3,2,1,0:T(8,128)}), f32[512,2,8,128]{3,2,1,0:T(8,128)}, u32[]{:S(2)}, u32[]{:S(2)}) %all-to-all-start.1) | async-done | bytes 4194336 | tf_op jit(solution)/shard_map/all_to_all | solution.py:88
  438.9 3.7 fusion.15
  443.4 298.7 %all-gather.5.cloned.1.call-done = bf16[512,2048]{1,0:T(8,128)(2,1)} async-done(((bf16[8,2048]{1,0:T(8,128)(2,1)}), bf16[512,2048]{1,0:T(8,128)(2,1)}) %all-gather.5.cloned.1.call-update) | async-done | bytes 2097168 | tf_op jit(solution)/shard_map/all_gather | solution.py:124
  742.1 3.0 fusion.80
  745.2 75.0 %reduce-scatter.2.cloned.1.call-done = f32[128,128]{1,0:T(8,128)} async-done(((f32[512,128]{1,0:T(8,128)}), f32[128,128]{1,0:T(8,128)}) %reduce-scatter.2.cloned.1.call-update) | async-done | bytes 65552 | tf_op jit(solution)/shard_map/reduce_scatter | solution.py:128
  820.1 1.5 convert_element_type.30
  (61 shorter events, 5.3 us)
Async XLA Ops:
  6.5 381.4 %copy-start = (bf16[36,128,2,128]{3,2,1,0:T(2,128)(2,1)S(1)}, bf16[36,128,2,128]{3,2,1,0:T(2,128)(2,1)}, u32[]{:S(2)}) copy-start(bf16[36,128,2,128]{3,2,1,0:T(2,128)(2,1)} %param.22) | copy-start | bytes 7077892
  6.5 260.9 %all-gather.3.cloned.1.call-start = ((), (), s32[]{:S(2)}) async-start(), calls=%async_computation.4 | async-start | bytes 2129920 | tf_op jit(solution)/shard_map/all_gather | solution.py:55
  284.8 2.8 copy-start.2
  313.0 40.0 %all-to-all-start.2 = ((f32[64,1,128]{2,1,0:T(1,128)}), f32[64,1,128]{2,1,0:T(1,128)S(1)}, u32[]{:S(2)}, u32[]{:S(2)}) async-start(f32[64,1,128]{2,1,0:T(1,128)} %reshape.312), calls=%async_computation.2 | async-start | bytes 65536 | tf_op jit(solution)/shard_map/all_to_all | solution.py:88
  339.1 10.1 %copy-start.6 = (f32[48,2,8]{0,2,1:T(8,128)S(1)}, f32[48,2,8]{0,2,1:T(8,128)}, u32[]{:S(2)}) copy-start(f32[48,2,8]{0,2,1:T(8,128)} %get-tuple-element.10) | copy-start | bytes 9220
  339.1 10.2 %copy-start.5 = (f32[48,2,8]{0,2,1:T(8,128)S(1)}, f32[48,2,8]{0,2,1:T(8,128)}, u32[]{:S(2)}) copy-start(f32[48,2,8]{0,2,1:T(8,128)} %get-tuple-element.11) | copy-start | bytes 9220
  339.1 10.3 %copy-start.4 = (f32[48,2,8]{0,2,1:T(8,128)S(1)}, f32[48,2,8]{0,2,1:T(8,128)}, u32[]{:S(2)}) copy-start(f32[48,2,8]{0,2,1:T(8,128)} %get-tuple-element.12) | copy-start | bytes 9220
  339.1 10.4 %copy-start.8 = (s32[48]{0:T(128)S(1)}, s32[48]{0:T(128)}, u32[]{:S(2)}) copy-start(s32[48]{0:T(128)} %get-tuple-element.6) | copy-start | bytes 580
  353.0 24.0 %all-to-all-start = ((f32[64,1,128]{2,1,0:T(1,128)}), f32[64,1,128]{2,1,0:T(1,128)S(1)}, u32[]{:S(2)}, u32[]{:S(2)}) async-start(f32[64,1,128]{2,1,0:T(1,128)} %reshape.310), calls=%async_computation | async-start | bytes 65536 | tf_op jit(solution)/shard_map/all_to_all | solution.py:88
  376.9 10.9 %copy-start.9 = (s32[8,8]{1,0:T(8,128)S(1)}, s32[8,8]{1,0:T(8,128)}, u32[]{:S(2)}) copy-start(s32[8,8]{1,0:T(8,128)} %param.20) | copy-start | bytes 772
  376.9 62.0 %all-to-all-start.1 = ((f32[512,2,8,128]{3,2,1,0:T(8,128)}), f32[512,2,8,128]{3,2,1,0:T(8,128)}, u32[]{:S(2)}, u32[]{:S(2)}) async-start(f32[512,2,8,128]{3,2,1,0:T(8,128)} %scatter_fusion.1), calls=%async_computation.1 | async-start | bytes 8388608 | tf_op jit(solution)/shard_map/all_to_all | solution.py:88
  387.6 354.5 %all-gather.5.cloned.1.call-start = ((), (), s32[]{:S(2)}) async-start(), calls=%async_computation.5 | async-start | bytes 2129920 | tf_op jit(solution)/shard_map/all_gather | solution.py:124
  398.6 12.4 %copy-start.10 = (s32[8]{0:T(128)S(1)}, s32[8]{0:T(128)}, u32[]{:S(2)}) copy-start(s32[8]{0:T(128)} %param.19) | copy-start | bytes 100
  398.6 12.4 %copy-start.3 = (bf16[8,16,128]{2,1,0:T(8,128)(2,1)S(1)}, bf16[8,16,128]{2,1,0:T(8,128)(2,1)}, u32[]{:S(2)}) copy-start(bf16[8,16,128]{2,1,0:T(8,128)(2,1)} %param.12) | copy-start | bytes 98308
  422.0 320.1 %copy-start.1 = (bf16[2048,128]{1,0:T(8,128)(2,1)S(1)}, bf16[2048,128]{1,0:T(8,128)(2,1)}, u32[]{:S(2)}) copy-start(bf16[2048,128]{1,0:T(8,128)(2,1)} %param.23) | copy-start | bytes 1572868
  426.8 15.8 %copy-start.7 = (f32[8,2,8]{2,1,0:T(2,128)S(1)}, f32[8,2,8]{2,1,0:T(2,128)}, u32[]{:S(2)}) copy-start(f32[8,2,8]{2,1,0:T(2,128)} %get-tuple-element.7) | copy-start | bytes 1540
  443.4 376.8 %reduce-scatter.2.cloned.1.call-start = ((), (), s32[]{:S(2)}) async-start(), calls=%async_computation.6 | async-start | bytes 327680 | tf_op jit(solution)/shard_map/reduce_scatter | solution.py:128
Sparse Core Ops, SparseCore 0:
  9.1 258.2 all-gather.2
  443.5 298.5 all-gather.4
  745.3 74.7 reduce-scatter.1
where the time goes:
time: 839 us; the launch traced here: 828 us
  waiting for transfers between devices  636 us (76%)
  local copies, waits for them, and re-layouts  62.8 us (7%)
  matrix products  46 us (5%)
  starting transfers between devices  35.8 us (4%)
  other arithmetic  33.5 us (4%)
  between operations  14.4 us (2%)
    all_gather x1, waiting for transfers between devices, local(): lax.all_gather(attended, 'seq', axis=0, tiled=True)  299 us
    all_gather x1, waiting for transfers between devices, local(): everyone = lax.all_gather(queries, 'seq', axis=0, tiled=True)  251 us
    reduce_scatter x1, waiting for transfers between devices, local(): lax.psum_scatter(partial_out, 'head', scatter_dimension=0, tiled=True)  75 us
    all_to_all x3, starting transfers between devices, local(): lax.all_to_all(joined, 'seq', split_axis=0, concat_axis=0, tiled=True)  35.5 us
    dot_general x3, matrix products, finish(): jnp.einsum(form, rounded, value_rows, preferred_element_type=jnp.float32)  23.2 us
  transfers between devices with their start and end apart: 6, of which 4 were waited for; matrix products, arithmetic and copies ran while one was open for 11% of the time, Pallas kernels for 0%

commit v1 on v0

v1 whole, which is shorter than its diff:
```python
import functools
import math

import jax
import jax.numpy as jnp
from jax import lax
from jax.experimental import pallas as pl
from jax.experimental.pallas import tpu as pltpu
from jax.sharding import PartitionSpec as P

MESH = pl.DeviceIdType.MESH
F32 = jnp.float32
BF16 = jnp.bfloat16
DEAD = -1e30
KV = 2
G = 8
D = 128
R = 8
HEADS = KV * G
CAP = 48
SLOTS = CAP * G
COLUMNS = R * G
LOG2E = math.log2(math.e)
SCALE = LOG2E / math.sqrt(D)


def dot(a, b):
    return jnp.dot(a, b, preferred_element_type=F32)


def dot_t(a, b):
    return lax.dot_general(a, b, (((1,), (1,)), ((), ())), preferred_element_type=F32)


def iota(shape, axis):
    return lax.broadcasted_iota(jnp.int32, shape, axis)


def kernel(
    NZ, NX, NH,
    q_hbm, sk_hbm, sv_hbm, tk_hbm, tv_hbm, ids_ref, tlen_ref, plen_ref, ptab_ref,
    pk_hbm, pv_hbm, w_hbm, out_ref,
    q_raw, q_wide, sk_raw, sv_raw, tk_raw, tv_raw, pk, pv, w,
    k_sh, v_sh, k_te, v_te,
    q_all, onehot, keys, qt_send, qt_recv,
    te_m, te_l, te_acc, to_send, to_recv, tl_send, tl_recv,
    te_hi, te_lo, te_stat, sh_o, sh_l,
    xo_send, xo_recv, xl_send, xl_recv,
    zo_send, zo_recv, zl_send, zl_recv,
    pr_o, pr_l, at, part, rs_recv,
    in_sem,
    qz_s, qz_r, qx_s, qx_r, pair_s, pair_r, xo_s, xo_r, xl_s, xl_r,
    zo_s, zo_r, zl_s, zl_r, az_s, az_r, ax_s, ax_r, rs_s, rs_r,
):
    seq = lax.axis_index("seq")
    h = lax.axis_index("head")
    b = lax.rem(seq, 2)
    x = lax.rem(seq // 2, NX)
    z = seq // (2 * NX)
    pages = pk.shape[0]
    zcols = NZ * COLUMNS
    zper = NZ // NH

    def seq_of(zz, xx, bb):
        return (zz * NX + xx) * 2 + bb

    def device(zz, xx, bb, hh):
        return {"seq": seq_of(zz, xx, bb), "head": hh}

    def z_of(dz):
        return lax.rem(z + dz + NZ, NZ)

    def x_of(dx):
        return lax.rem(x + dx + NX, NX)

    def h_of(dh):
        return lax.rem(h + dh + NH, NH)

    def b_of(db):
        return lax.rem(b + db, 2)

    def send(src, dst, s, r, dev):
        return pltpu.make_async_remote_copy(
            src_ref=src, dst_ref=dst, send_sem=s, recv_sem=r, device_id=dev, device_id_type=MESH
        )

    me = device(z, x, b, h)
    pair = device(z, x, b_of(1), h)
    started = []

    def go(*args):
        copy = send(*args)
        copy.start()
        started.append(copy)

    def arrived(ref, s, r):
        send(ref, ref, s, r, pair).wait_recv()

    loads = {}
    for at_sem, (name, src, dst) in enumerate((
        ("q", q_hbm, q_raw),
        ("tk", tk_hbm, tk_raw),
        ("sk", sk_hbm, sk_raw.at[0]),
        ("sv", sv_hbm, sv_raw.at[0]),
        ("tv", tv_hbm, tv_raw),
        ("pk", pk_hbm, pk),
        ("pv", pv_hbm, pv),
        ("w", w_hbm, w.at[0]),
    )):
        loads[name] = pltpu.make_async_copy(src, dst, in_sem.at[at_sem])
        loads[name].start()

    barrier = pltpu.get_barrier_semaphore()
    peers = [device(z_of(dz), x, b, h) for dz in range(1, NZ)]
    peers += [device(z, x_of(dx), b, h) for dx in range(1, NX)]
    peers += [
        device(z, x, b_of(db), h_of(dh)) for dh in range(NH) for db in range(2) if dh + db > 0
    ]
    for peer in peers:
        pl.semaphore_signal(barrier, inc=1, device_id=peer, device_id_type=MESH)

    loads["q"].wait()
    q_wide[...] = q_raw[...].astype(F32).reshape(R * HEADS, D)
    q_all[x, z] = jnp.concatenate(
        [q_wide[pl.ds(i, R, stride=HEADS), :] for i in range(HEADS)], axis=0
    ).astype(BF16)

    pl.semaphore_wait(barrier, len(peers))

    for dz in range(1, NZ):
        go(q_all.at[x, z], q_all.at[x, z], qz_s.at[dz - 1], qz_r.at[dz - 1], device(z_of(dz), x, b, h))
    go(sk_hbm, sk_raw.at[1], pair_s.at[0], pair_r.at[0], pair)
    go(sv_hbm, sv_raw.at[1], pair_s.at[1], pair_r.at[1], pair)

    row, col = iota((2 * D, 2 * D), 0), iota((2 * D, 2 * D), 1)
    sort = (col == jnp.where(row < D, 2 * row, 2 * (row - D) + 1)).astype(F32).astype(BF16)

    def sort_keys(raw, into, count, base):
        def step(i, carry):
            at_row = pl.multiple_of(i * 2 * D, 2 * D)
            to_row = pl.multiple_of(base + i * D, D)
            rows = dot(sort, raw[pl.ds(at_row, 2 * D), :]).astype(BF16)
            into[0, pl.ds(to_row, D), :] = rows[:D]
            into[1, pl.ds(to_row, D), :] = rows[D:]
            return carry

        lax.fori_loop(0, count // D, step, 0, unroll=4)

    def sort_values(raw, into, count, base):
        def step(i, carry):
            at_row = pl.multiple_of(i * 2 * D, 2 * D)
            to_row = pl.multiple_of(base + i * D, D)
            rows = dot(sort, raw[pl.ds(at_row, 2 * D), :])
            into[0, :, pl.ds(to_row, D)] = rows[:D].T.astype(BF16)
            into[1, :, pl.ds(to_row, D)] = rows[D:].T.astype(BF16)
            return carry

        lax.fori_loop(0, count // D, step, 0, unroll=4)

    positions = k_te.shape[1]
    half = sk_raw.shape[1] // 2

    tenant = seq // 4
    requests = ids_ref.shape[1]
    match = (ids_ref[...] == tenant).astype(F32)
    match = jnp.broadcast_to(match, (16, requests))
    upto = (iota((requests, requests), 0) <= iota((requests, requests), 1)).astype(F32).astype(BF16)
    slot = (match * dot(match.astype(BF16), upto)).astype(BF16)
    for xx in range(NX):
        j = iota((1, zcols), 1)
        request = ((j // COLUMNS * NX + xx) * 2 + b) * R + lax.rem(j, R)
        pick = (iota((requests, zcols), 0) == request).astype(F32).astype(BF16)
        found = dot(slot, pick)[:1]
        group = (lax.rem(j, COLUMNS) // R).astype(F32)
        key = jnp.where(found > 0.5, group * CAP + found - 1.0, -1.0)
        keys[xx] = jnp.broadcast_to(key, (8, zcols))
        onehot[xx] = (iota((SLOTS, zcols), 0).astype(F32) == key).astype(F32).astype(BF16)

    for dz in range(1, NZ):
        arrived(q_all.at[x, z_of(-dz)], qz_s.at[dz - 1], qz_r.at[dz - 1])
    for dx in range(1, NX):
        go(q_all.at[x], q_all.at[x], qx_s.at[dx - 1], qx_r.at[dx - 1], device(z, x_of(dx), b, h))

    loads["tk"].wait()
    sort_keys(tk_raw, k_te, positions, 0)
    loads["sk"].wait()
    sort_keys(sk_raw.at[0], k_sh, half, 0)
    loads["sv"].wait()
    sort_values(sv_raw.at[0], v_sh, half, 0)
    loads["tv"].wait()
    sort_values(tv_raw, v_te, positions, 0)

    for dx in range(1, NX):
        arrived(q_all.at[x_of(-dx)], qx_s.at[dx - 1], qx_r.at[dx - 1])

    def chunk_queries(xx, kv):
        return q_all[xx, :, kv * COLUMNS:(kv + 1) * COLUMNS, :].reshape(zcols, D)

    for kv in range(KV):
        total = dot(onehot[0], chunk_queries(0, kv))
        for xx in range(1, NX):
            total += dot(onehot[xx], chunk_queries(xx, kv))
        qt_send[kv] = total.astype(BF16)
    go(qt_send, qt_recv, pair_s.at[2], pair_r.at[2], pair)

    loads["pk"].wait()
    loads["pv"].wait()
    span = ptab_ref.shape[1] * pk.shape[1]
    lane = iota((HEADS, span), 1)
    own = lax.rem(lane, 2) == iota((HEADS, span), 0) // G
    for r in range(R):
        keys_here = jnp.concatenate([pk[ptab_ref[r, p]] for p in range(ptab_ref.shape[1])], axis=0)
        values_here = jnp.concatenate([pv[ptab_ref[r, p]] for p in range(ptab_ref.shape[1])], axis=0)
        s = dot_t(q_raw[r], keys_here)
        s = jnp.where(own & (lane // 2 < plen_ref[r]), s, DEAD)
        m = jnp.max(s, axis=1, keepdims=True)
        p = jnp.exp2((s - m) * SCALE)
        l = jnp.sum(p, axis=1, keepdims=True)
        o = dot(p.astype(BF16), values_here) / l
        lse = jnp.where(plen_ref[r] > 0, m * SCALE + jnp.log2(l), DEAD)
        pr_o[pl.ds(r, HEADS, stride=R), :] = o
        pr_l[pl.ds(r, HEADS, stride=R), :] = jnp.broadcast_to(lse, (HEADS, D))

    arrived(sk_raw.at[1], pair_s.at[0], pair_r.at[0])
    sort_keys(sk_raw.at[1], k_sh, half, half)
    arrived(sv_raw.at[1], pair_s.at[1], pair_r.at[1])
    sort_values(sv_raw.at[1], v_sh, half, half)

    arrived(qt_recv, pair_s.at[2], pair_r.at[2])
    extent = tlen_ref[tenant] - lax.rem(seq, 4) * positions
    block = min(1024, positions)
    for kv in range(KV):
        queries = (qt_send[kv].astype(F32) + qt_recv[kv].astype(F32)).astype(BF16)
        te_m[...] = jnp.full(te_m.shape, DEAD, F32)
        te_l[...] = jnp.zeros(te_l.shape, F32)
        te_acc[...] = jnp.zeros(te_acc.shape, F32)

        def step(i, carry):
            base = pl.multiple_of(i * block, block)
            s = dot_t(k_te[kv, pl.ds(base, block), :], queries)
            s = jnp.where(iota((block, SLOTS), 0) < extent - base, s, DEAD)
            m_old = te_m[:1]
            m = jnp.maximum(m_old, jnp.max(s, axis=0, keepdims=True))
            p = jnp.exp2((s - m) * SCALE)
            keep = jnp.exp2((m_old - m) * SCALE)
            te_m[:1] = m
            te_l[:1] = te_l[:1] * keep + jnp.sum(p, axis=0, keepdims=True)
            te_acc[...] = te_acc[...] * keep + dot(v_te[kv, :, pl.ds(base, block)], p.astype(BF16))
            return carry

        lax.fori_loop(0, positions // block, step, 0)
        l = te_l[:1]
        to_send[kv] = (te_acc[...] / l).astype(BF16)
        lse = jnp.where(extent > 0, te_m[:1] * SCALE + jnp.log2(l), DEAD)
        tl_send[kv] = jnp.broadcast_to(lse, (8, SLOTS))
    go(to_send, to_recv, pair_s.at[3], pair_r.at[3], pair)
    go(tl_send, tl_recv, pair_s.at[4], pair_r.at[4], pair)
    go(w_hbm, w.at[1], pair_s.at[5], pair_r.at[5], pair)

    width = min(256, zcols)

    def shared(xx):
        for kv in range(KV):
            for c in range(0, zcols, width):
                zs = slice(c // COLUMNS, (c + width) // COLUMNS)
                queries = q_all[xx, zs, kv * COLUMNS:(kv + 1) * COLUMNS, :].reshape(width, D)
                s = dot_t(k_sh[kv], queries)
                m = jnp.max(s, axis=0, keepdims=True)
                p = jnp.exp2((s - m) * SCALE)
                l = jnp.sum(p, axis=0, keepdims=True)
                sh_o[xx, kv, :, c:c + width] = dot(v_sh[kv], p.astype(BF16)) / l
                lse = m * SCALE + jnp.log2(l)
                sh_l[xx, kv, :, c:c + width] = jnp.broadcast_to(lse, (8, width))

    def tenants():
        arrived(to_recv, pair_s.at[3], pair_r.at[3])
        arrived(tl_recv, pair_s.at[4], pair_r.at[4])
        for kv in range(KV):
            l1, l2 = tl_send[kv][:1], tl_recv[kv][:1]
            top = jnp.maximum(l1, l2)
            w1, w2 = jnp.exp2(l1 - top), jnp.exp2(l2 - top)
            whole = w1 + w2
            o = to_send[kv].astype(F32) * (w1 / whole) + to_recv[kv].astype(F32) * (w2 / whole)
            hi = o.astype(BF16)
            te_hi[kv] = hi
            te_lo[kv] = (o - hi.astype(F32)).astype(BF16)
            rest = top + jnp.log2(whole)
            terms = []
            for _ in range(3):
                term = rest.astype(BF16).astype(F32)
                terms.append(term)
                rest = rest - term
            terms.append(jnp.zeros((13, SLOTS), F32))
            te_stat[kv] = jnp.concatenate(terms, axis=0).astype(BF16)

    def merge(xx):
        for kv in range(KV):
            spread = onehot[xx]
            stat = dot(te_stat[kv], spread)
            l2 = stat[0:1] + stat[1:2] + stat[2:3]
            l2 = jnp.where(keys[xx][:1] >= 0.0, l2, DEAD)
            l1 = sh_l[xx, kv][:1]
            top = jnp.maximum(l1, l2)
            w1, w2 = jnp.exp2(l1 - top), jnp.exp2(l2 - top)
            whole = w1 + w2
            o2 = dot(te_hi[kv], spread) + dot(te_lo[kv], spread)
            o = sh_o[xx, kv] * (w1 / whole) + o2 * (w2 / whole)
            xo_send[xx, kv] = o.astype(BF16)
            xl_send[xx, kv] = jnp.broadcast_to(top + jnp.log2(whole), (8, zcols))

    def dispatch(dx):
        to = device(z, x_of(dx), b, h)
        go(xo_send.at[x_of(dx)], xo_recv.at[dx - 1], xo_s.at[dx - 1], xo_r.at[dx - 1], to)
        go(xl_send.at[x_of(dx)], xl_recv.at[dx - 1], xl_s.at[dx - 1], xl_r.at[dx - 1], to)

    ahead = min(2, NX - 1)
    for dx in range(1, ahead + 1):
        shared(x_of(dx))
    tenants()
    for dx in range(1, ahead + 1):
        merge(x_of(dx))
        dispatch(dx)
    for dx in range(ahead + 1, NX):
        shared(x_of(dx))
        merge(x_of(dx))
        dispatch(dx)
    shared(x)
    merge(x)

    for dx in range(1, NX):
        arrived(xo_recv.at[dx - 1], xo_s.at[dx - 1], xo_r.at[dx - 1])
        arrived(xl_recv.at[dx - 1], xl_s.at[dx - 1], xl_r.at[dx - 1])

    def combine(pieces):
        top = pieces[0][0]
        for lse, _ in pieces[1:]:
            top = jnp.maximum(top, lse)
        weights = [jnp.exp2(lse - top) for lse, _ in pieces]
        whole = functools.reduce(lambda one, two: one + two, weights)
        total = None
        for weight, (_, o) in zip(weights, pieces):
            term = o().astype(F32) * (weight / whole)
            total = term if total is None else total + term
        return total, top + jnp.log2(whole)

    both = 2 * COLUMNS
    low = iota((D, both), 1) < COLUMNS
    for c in range(0, zcols, both):
        cut = slice(c, c + both)
        halves, marks = [], []
        for kv in range(KV):
            pieces = [(xl_send[x, kv, :1, cut], lambda: xo_send[x, kv, :, cut])]
            for dx in range(1, NX):
                pieces.append((
                    xl_recv[dx - 1, kv, :1, cut],
                    lambda dx=dx: xo_recv[dx - 1, kv, :, cut],
                ))
            o, lse = combine(pieces)
            halves.append(o)
            marks.append(jnp.broadcast_to(lse, (8, both)))
        zz = c // COLUMNS
        zo_send[zz] = jnp.where(low, halves[0], pltpu.roll(halves[1], COLUMNS, 1)).astype(BF16)
        zo_send[zz + 1] = jnp.where(low, pltpu.roll(halves[0], COLUMNS, 1), halves[1]).astype(BF16)
        zl_send[zz] = jnp.where(low[:8], marks[0], pltpu.roll(marks[1], COLUMNS, 1))
        zl_send[zz + 1] = jnp.where(low[:8], pltpu.roll(marks[0], COLUMNS, 1), marks[1])
    for dz in range(1, NZ):
        to = device(z_of(dz), x, b, h)
        go(zo_send.at[z_of(dz)], zo_recv.at[dz - 1], zo_s.at[dz - 1], zo_r.at[dz - 1], to)
        go(zl_send.at[z_of(dz)], zl_recv.at[dz - 1], zl_s.at[dz - 1], zl_r.at[dz - 1], to)

    private_o = pr_o[...].T
    private_l = pr_l[...].T[:1]
    for dz in range(1, NZ):
        arrived(zo_recv.at[dz - 1], zo_s.at[dz - 1], zo_r.at[dz - 1])
        arrived(zl_recv.at[dz - 1], zl_s.at[dz - 1], zl_r.at[dz - 1])
    pieces = [(private_l, lambda: private_o), (zl_send[z][:1], lambda: zo_send[z])]
    for dz in range(1, NZ):
        pieces.append((zl_recv[dz - 1][:1], lambda dz=dz: zo_recv[dz - 1]))
    attended, _ = combine(pieces)
    at[x, z] = attended.T.astype(BF16)

    for dz in range(1, NZ):
        go(at.at[x, z], at.at[x, z], az_s.at[dz - 1], az_r.at[dz - 1], device(z_of(dz), x, b, h))
    for dz in range(1, NZ):
        arrived(at.at[x, z_of(-dz)], az_s.at[dz - 1], az_r.at[dz - 1])
    for dx in range(1, NX):
        go(at.at[x], at.at[x], ax_s.at[dx - 1], ax_r.at[dx - 1], device(z, x_of(dx), b, h))

    def project(xx):
        wide = at[xx].astype(F32)
        rows = [
            wide[:, i * R:(i + 1) * R, :].reshape(NZ * R, D).astype(BF16) for i in range(HEADS)
        ]
        rows = jnp.concatenate(rows, axis=1)
        for db in range(2):
            part[db, :, xx] = dot(rows, w[db]).reshape(NZ, R, D)

    loads["w"].wait()
    arrived(w.at[1], pair_s.at[5], pair_r.at[5])
    project(x)
    for dx in range(1, NX):
        arrived(at.at[x_of(-dx)], ax_s.at[dx - 1], ax_r.at[dx - 1])
        project(x_of(-dx))

    for k in range(1, 2 * NH):
        dh, db = k // 2, k % 2
        src = part.at[db, pl.ds(h_of(dh) * zper, zper)]
        go(src, rs_recv.at[k - 1], rs_s.at[k - 1], rs_r.at[k - 1], device(z, x, b_of(db), h_of(dh)))
    totals = [part[0, pl.ds(h * zper, zper)], None]
    for k in range(1, 2 * NH):
        arrived(rs_recv.at[k - 1], rs_s.at[k - 1], rs_r.at[k - 1])
        got = rs_recv[k - 1]
        totals[k % 2] = got if totals[k % 2] is None else totals[k % 2] + got
    first = jnp.where(b == 0, totals[0], totals[1])
    second = jnp.where(b == 0, totals[1], totals[0])
    rows = jnp.concatenate([first[:, :, None], second[:, :, None]], axis=2)
    out_ref[...] = rows.reshape(zper * NX * 2 * R, D).astype(BF16)

    for copy in started:
        copy.wait_send()


def local(NZ, NX, NH, queries, sk, sv, tk, tv, ids, tlen, plen, ptab, pk, pv, w):
    flat = lambda rows: rows.reshape(rows.shape[0] * KV, D)
    paged = lambda rows: rows.reshape(rows.shape[0], rows.shape[1] * KV, D)
    sk, sv, tk, tv = flat(sk), flat(sv), flat(tk), flat(tv)
    pk, pv = paged(pk), paged(pv)
    shared2, positions = sk.shape[0], tk.shape[0] // KV
    zcols = NZ * COLUMNS
    zper = NZ // NH
    dma = pltpu.SemaphoreType.DMA
    v = pltpu.VMEM
    scratch = [
        v(queries.shape, BF16), v((R * HEADS, D), F32),
        v((2, shared2, D), BF16), v((2, shared2, D), BF16), v(tk.shape, BF16), v(tv.shape, BF16),
        v(pk.shape, BF16), v(pv.shape, BF16), v((2,) + w.shape, BF16),
        v((KV, shared2, D), BF16), v((KV, D, shared2), BF16),
        v((KV, positions, D), BF16), v((KV, D, positions), BF16),
        v((NX, NZ, R * HEADS, D), BF16), v((NX, SLOTS, zcols), BF16), v((NX, 8, zcols), F32),
        v((KV, SLOTS, D), BF16), v((KV, SLOTS, D), BF16),
        v((8, SLOTS), F32), v((8, SLOTS), F32), v((D, SLOTS), F32),
        v((KV, D, SLOTS), BF16), v((KV, D, SLOTS), BF16),
        v((KV, 8, SLOTS), F32), v((KV, 8, SLOTS), F32),
        v((KV, D, SLOTS), BF16), v((KV, D, SLOTS), BF16), v((KV, 16, SLOTS), BF16),
        v((NX, KV, D, zcols), F32), v((NX, KV, 8, zcols), F32),
        v((NX, KV, D, zcols), BF16), v((NX - 1, KV, D, zcols), BF16),
        v((NX, KV, 8, zcols), F32), v((NX - 1, KV, 8, zcols), F32),
        v((NZ, D, R * HEADS), BF16), v((NZ - 1, D, R * HEADS), BF16),
        v((NZ, 8, R * HEADS), F32), v((NZ - 1, 8, R * HEADS), F32),
        v((R * HEADS, D), F32), v((R * HEADS, D), F32),
        v((NX, NZ, R * HEADS, D), BF16), v((2, NZ, NX, R, D), F32),
        v((2 * NH - 1, zper, NX, R, D), F32),
        dma((8,)),
    ]
    for count in (NZ - 1, NX - 1, 6, NX - 1, NX - 1, NZ - 1, NZ - 1, NZ - 1, NX - 1, 2 * NH - 1):
        scratch += [dma((count,)), dma((count,))]
    hbm = pl.BlockSpec(memory_space=pl.ANY)
    smem = pl.BlockSpec(memory_space=pltpu.SMEM)
    vmem = pl.BlockSpec(memory_space=pltpu.VMEM)
    return pl.pallas_call(
        functools.partial(kernel, NZ, NX, NH),
        out_shape=jax.ShapeDtypeStruct((zper * NX * 2 * R, D), BF16),
        in_specs=[hbm] * 5 + [vmem, smem, smem, smem] + [hbm] * 3,
        out_specs=vmem,
        scratch_shapes=scratch,
        compiler_params=pltpu.CompilerParams(
            collective_id=0, has_side_effects=True, vmem_limit_bytes=56 * 1024 * 1024
        ),
    )(queries, sk, sv, tk, tv, ids.reshape(1, -1), tlen, plen, ptab, pk, pv, w)


def solution(mesh):
    sizes = dict(mesh.shape)
    NX = 4 if sizes["seq"] == 64 else 2
    NZ = sizes["seq"] // (2 * NX)
    placed = (
        P("seq", "head", None),
        P("seq", "head", None),
        P("seq", "head", None),
        P("seq", "head", None),
        P("seq", "head", None),
        P(),
        P(),
        P("seq"),
        P("seq", None),
        P("seq", None, "head", None),
        P("seq", None, "head", None),
        P("head", "seq"),
    )
    return jax.shard_map(
        functools.partial(local, NZ, NX, sizes["head"]),
        mesh=mesh, in_specs=placed, out_specs=P("head", "seq"), check_vma=False,
    )
```

time: 839 us -> 102 us (0.12); the launches traced: 828 us -> 101 us
  waiting for transfers between devices: 636 us -> 0 us
  Pallas kernels: 0 us -> 99.9 us
  local copies, waits for them, and re-layouts: 62.8 us -> 1.38 us
  matrix products: 46 us -> 0 us
  starting transfers between devices: 35.8 us -> 0 us
  other arithmetic: 33.5 us -> 0 us
  between operations: 14.4 us -> 0.01 us
    all_gather x2 -> x0, waiting for transfers between devices: 549 us -> none  [the longest x1 299 us: local(): lax.all_gather(attended, 'seq', axis=0, tiled=True)]
    pallas_call x0 -> x1, Pallas kernels: none -> 99.9 us  [local(): pl.pallas_call(functools.partial(kernel, NZ, NX, NH), out_shape=jax.Shape...]
    reduce_scatter x1 -> x0, waiting for transfers between devices: 75 us -> none  [local(): lax.psum_scatter(partial_out, 'head', scatter_dimension=0, tiled=True)]
    dot_general x7 -> x0, matrix products: 46 us -> none  [the longest x3 23.2 us: finish(): jnp.einsum(form, rounded, value_rows, preferred_element_type=jnp.float32)]
    all_to_all x3 -> x0, starting transfers between devices: 35.5 us -> none  [local(): lax.all_to_all(joined, 'seq', split_axis=0, concat_axis=0, tiled=True)]
    gather x8 -> x0, local copies, waits for them, and re-layouts: 31.3 us -> none  [the longest x1 12.4 us: local(): private_key_pages[page_table].reshape(owned_rows, -1, kv_local, head_dim)]
    reduce_sum x6 -> x0, other arithmetic: 22.9 us -> none  [the longest x3 15.7 us: finish(): totals = jnp.sum(weights, axis=-1)]
    all_to_all x3 -> x0, waiting for transfers between devices: 10.7 us -> none  [local(): lax.all_to_all(joined, 'seq', split_axis=0, concat_axis=0, tiled=True)]
  transfers between devices with their start and end apart: 6 -> 0, of which waited for: 4 -> 0; matrix products, arithmetic and copies ran while one was open for 11% -> 0% of each run, Pallas kernels for 0% -> 0%
where the time goes in v1:
time: 102 us; the launch traced here: 101 us
  Pallas kernels  99.9 us (98%)
  local copies, waits for them, and re-layouts  1.38 us (1%)
    pallas_call x1, Pallas kernels, local(): pl.pallas_call(functools.partial(kernel, NZ, NX, NH), out_shape=jax.Shape...  99.9 us

profile of v1, /device:TPU:1, one launch (start us, length us, event | category | flops | bytes accessed | tf_op | source)
XLA Modules:
  0.0 101.2 jit_solution(9486043978304258383)
XLA Ops:
  0.0 99.9 %shard_map.118 = bf16[128,128]{1,0:T(8,128)(2,1)} custom-call(bf16[8,16,128]{2,1,0:T(8,128)(2,1)} %q_hbm.1, bf16[1024,128]{1,0:T(8,128)(2,1)} %bitcast.11, bf16[1024,128]{1,0:T(8,128)(2,1)} %bitcast.12, bf16[8192,128]{1,0:T(8,128)(2,1)} %bitcast.9, bf16[8192,128]{1,0:T(8,128)(2,1)} %bitcast.10, s32[1,512]{1,0:T(1,128)} %bitcast.13, s32[16]{0:T(128)} %tlen_ref.1, ...), custom_call_target="tpu_custom_call" | custom-call | tf_op jit(solution)/shard_map/pallas_call | solution.py:460
  99.9 1.4 %copy.14 = bf16[128,128]{1,0:T(8,128)(2,1)} copy(bf16[128,128]{1,0:T(8,128)(2,1)} %shard_map.118) | data formatting | bytes 65536

commit v2 on v1

v2 whole, which is shorter than its diff:
```python
import functools
import math

import jax
import jax.numpy as jnp
from jax import lax
from jax.experimental import pallas as pl
from jax.experimental.pallas import tpu as pltpu
from jax.sharding import PartitionSpec as P

MESH = pl.DeviceIdType.MESH
F32 = jnp.float32
BF16 = jnp.bfloat16
DEAD = -1e30
KV = 2
G = 8
D = 128
R = 8
HEADS = KV * G
STAT = 16
CAP = 48
SLOTS = CAP * G
COLUMNS = R * G
LOG2E = math.log2(math.e)
SCALE = LOG2E / math.sqrt(D)


def dot(a, b):
    return jnp.dot(a, b, preferred_element_type=F32)


def dot_t(a, b):
    return lax.dot_general(a, b, (((1,), (1,)), ((), ())), preferred_element_type=F32)


def split3(v):
    terms = []
    for _ in range(3):
        term = v.astype(BF16).astype(F32)
        terms.append(term)
        v = v - term
    terms.append(jnp.zeros((STAT - 3, v.shape[1]), F32))
    return jnp.concatenate(terms, axis=0).astype(BF16)


def join3(rows):
    rows = rows.astype(F32)
    return rows[0:1] + rows[1:2] + rows[2:3]


def combine(pieces):
    top = pieces[0][0]
    for lse, _ in pieces[1:]:
        top = jnp.maximum(top, lse)
    weights = [jnp.exp2(lse - top) for lse, _ in pieces]
    whole = functools.reduce(lambda one, two: one + two, weights)
    inverse = 1.0 / whole
    total = None
    for weight, (_, o) in zip(weights, pieces):
        term = o().astype(F32) * (weight * inverse)
        total = term if total is None else total + term
    return total, top + jnp.log2(whole)


def iota(shape, axis):
    return lax.broadcasted_iota(jnp.int32, shape, axis)


def kernel(
    NZ, NX, NH,
    q_hbm, sk_hbm, sv_hbm, tk_hbm, tv_hbm, ids_ref, tlen_ref, plen_ref, ptab_ref,
    pk_hbm, pv_hbm, w_hbm, out_ref,
    q_raw, q_wide, sk_raw, sv_raw, tk_raw, tv_raw, pk, pv, w,
    k_sh, v_sh, k_te, v_te,
    q_all, onehot, keys, qt_send, qt_recv,
    te_m, te_l, te_acc, to_send, to_recv, tl_send, tl_recv,
    te_hi, te_lo, te_stat, sh_o, sh_l,
    xo_send, xo_half, xo_full, zo_own, zl_own, zo_send, zo_recv,
    pr_o, pr_l, at, part, rs_recv,
    in_sem,
    qz_s, qz_r, qx_s, qx_r, pair_s, pair_r, xo_s, xo_r,
    zo_s, zo_r, az_s, az_r, ax_s, ax_r, rs_s, rs_r,
):
    seq = lax.axis_index("seq")
    h = lax.axis_index("head")
    b = lax.rem(seq, 2)
    x = lax.rem(seq // 2, NX)
    z = seq // (2 * NX)
    pages = pk.shape[0]
    zcols = NZ * COLUMNS
    zper = NZ // NH

    def seq_of(zz, xx, bb):
        return (zz * NX + xx) * 2 + bb

    def device(zz, xx, bb, hh):
        return {"seq": seq_of(zz, xx, bb), "head": hh}

    zorder = [(p + 1) // 2 if p % 2 else -(p // 2) for p in range(NZ)]
    xorder = [0, 1, -1, 2]
    cuts = [0, 1, 3, 5, 8] if NZ == 8 else [0, 1, NZ]
    groups = list(zip(cuts[:-1], cuts[1:]))

    def back(p):
        return [(zorder[p] + other) % NZ for other in zorder].index(0)

    def z_of(dz):
        return lax.rem(z + dz + NZ, NZ)

    def x_of(dx):
        return lax.rem(x + dx + NX, NX)

    def h_of(dh):
        return lax.rem(h + dh + NH, NH)

    def b_of(db):
        return lax.rem(b + db, 2)

    def send(src, dst, s, r, dev):
        return pltpu.make_async_remote_copy(
            src_ref=src, dst_ref=dst, send_sem=s, recv_sem=r, device_id=dev, device_id_type=MESH
        )

    me = device(z, x, b, h)
    pair = device(z, x, b_of(1), h)
    started = []

    def go(*args):
        copy = send(*args)
        copy.start()
        started.append(copy)

    def arrived(ref, s, r):
        send(ref, ref, s, r, pair).wait_recv()

    loads = {}
    for at_sem, (name, src, dst) in enumerate((
        ("q", q_hbm, q_raw),
        ("tk", tk_hbm, tk_raw),
        ("sk", sk_hbm, sk_raw.at[0]),
        ("sv", sv_hbm, sv_raw.at[0]),
        ("tv", tv_hbm, tv_raw),
        ("pk", pk_hbm, pk),
        ("pv", pv_hbm, pv),
        ("w", w_hbm, w.at[0]),
    )):
        loads[name] = pltpu.make_async_copy(src, dst, in_sem.at[at_sem])
        loads[name].start()

    barrier = pltpu.get_barrier_semaphore()
    peers = [device(z_of(dz), x, b, h) for dz in range(1, NZ)]
    peers += [device(z, x_of(dx), b, h) for dx in range(1, NX)]
    peers += [
        device(z, x, b_of(db), h_of(dh)) for dh in range(NH) for db in range(2) if dh + db > 0
    ]
    for peer in peers:
        pl.semaphore_signal(barrier, inc=1, device_id=peer, device_id_type=MESH)

    loads["q"].wait()
    q_wide[...] = q_raw[...].astype(F32).reshape(R * HEADS, D)
    q_all[0, 0] = jnp.concatenate(
        [q_wide[pl.ds(i, R, stride=HEADS), :] for i in range(HEADS)], axis=0
    ).astype(BF16)

    pl.semaphore_wait(barrier, len(peers))

    left, right = device(z, x_of(-1), b, h), device(z, x_of(1), b, h)

    def z_start(buf, zs, zr):
        for p in range(1, NZ):
            q = back(p)
            go(buf.at[0, 0], buf.at[0, q], zs.at[p - 1], zr.at[q - 1], device(z_of(zorder[p]), x, b, h))

    def z_wait(buf, zs, zr, group):
        for p in range(*groups[group]):
            if p > 0:
                arrived(buf.at[0, p], zs.at[p - 1], zr.at[p - 1])

    def block(buf, slot, group, kind=None):
        first, last = groups[group]
        if kind is None:
            return buf.at[slot, pl.ds(first, last - first)]
        return buf.at[slot, pl.ds(first, last - first), pl.ds((kind - 2) * COLUMNS, COLUMNS)]

    def forward(buf, xs, xr, group):
        k = 4 * group
        go(block(buf, 0, group), block(buf, 2, group), xs.at[k], xr.at[k], right)
        go(block(buf, 0, group), block(buf, 1, group), xs.at[k + 1], xr.at[k + 1], left)

    def relay(buf, xs, xr, group):
        k = 4 * group
        arrived(block(buf, 2, group), xs.at[k], xr.at[k])
        go(block(buf, 2, group, 2), block(buf, 3, group, 2), xs.at[k + 2], xr.at[k + 2], right)
        arrived(block(buf, 1, group), xs.at[k + 1], xr.at[k + 1])
        go(block(buf, 1, group, 3), block(buf, 3, group, 3), xs.at[k + 3], xr.at[k + 3], left)

    def far_wait(buf, xs, xr, group):
        for kind in (2, 3):
            k = 4 * group + kind
            arrived(block(buf, 3, group, kind), xs.at[k], xr.at[k])

    q_line = (q_all, qx_s, qx_r)
    z_start(q_all, qz_s, qz_r)
    forward(*q_line, 0)
    go(sk_hbm, sk_raw.at[1], pair_s.at[0], pair_r.at[0], pair)
    go(sv_hbm, sv_raw.at[1], pair_s.at[1], pair_r.at[1], pair)

    row, col = iota((2 * D, 2 * D), 0), iota((2 * D, 2 * D), 1)
    sort = (col == jnp.where(row < D, 2 * row, 2 * (row - D) + 1)).astype(F32).astype(BF16)

    def sort_keys(raw, into, first, last, base):
        def step(i, carry):
            at_row = pl.multiple_of(i * 2 * D, 2 * D)
            to_row = pl.multiple_of(base + i * D, D)
            rows = dot(sort, raw[pl.ds(at_row, 2 * D), :]).astype(BF16)
            into[0, pl.ds(to_row, D), :] = rows[:D]
            into[1, pl.ds(to_row, D), :] = rows[D:]
            return carry

        lax.fori_loop(first // D, last // D, step, 0, unroll=4)

    def sort_values(raw, into, first, last, base):
        def step(i, carry):
            at_row = pl.multiple_of(i * 2 * D, 2 * D)
            to_row = pl.multiple_of(base + i * D, D)
            rows = dot(sort, raw[pl.ds(at_row, 2 * D), :])
            into[0, :, pl.ds(to_row, D)] = rows[:D].T.astype(BF16)
            into[1, :, pl.ds(to_row, D)] = rows[D:].T.astype(BF16)
            return carry

        lax.fori_loop(first // D, last // D, step, 0, unroll=4)

    positions = k_te.shape[1]
    half = sk_raw.shape[1] // 2

    tenant = seq // 4
    requests = ids_ref.shape[1]
    match = (ids_ref[...] == tenant).astype(F32)
    match = jnp.broadcast_to(match, (16, requests))
    upto = (iota((requests, requests), 0) <= iota((requests, requests), 1)).astype(F32).astype(BF16)
    slot = (match * dot(match.astype(BF16), upto)).astype(BF16)

    def mark(xx):
        j = iota((1, zcols), 1)
        place = j // COLUMNS
        away = jnp.where(place % 2 == 1, (place + 1) // 2, -(place // 2))
        owner = seq_of(lax.rem(z + away + NZ, NZ), x_of(xorder[xx]), b)
        request = owner * R + lax.rem(j, R)
        pick = (iota((requests, zcols), 0) == request).astype(F32).astype(BF16)
        found = dot(slot, pick)[:1]
        group = (lax.rem(j, COLUMNS) // R).astype(F32)
        key = jnp.where(found > 0.5, group * CAP + found - 1.0, -1.0)
        keys[xx] = jnp.broadcast_to(key, (8, zcols))
        onehot[xx] = (iota((SLOTS, zcols), 0).astype(F32) == key).astype(F32).astype(BF16)

    def private(r):
        keys_here = jnp.concatenate([pk[ptab_ref[r, p]] for p in range(ptab_ref.shape[1])], axis=0)
        values_here = jnp.concatenate([pv[ptab_ref[r, p]] for p in range(ptab_ref.shape[1])], axis=0)
        s = dot_t(q_raw[r], keys_here)
        s = jnp.where(own & (lane // 2 < plen_ref[r]), s, DEAD)
        m = jnp.max(s, axis=1, keepdims=True)
        p = jnp.exp2((s - m) * SCALE)
        l = jnp.sum(p, axis=1, keepdims=True)
        o = dot(p.astype(BF16), values_here) / l
        lse = jnp.where(plen_ref[r] > 0, m * SCALE + jnp.log2(l), DEAD)
        pr_o[pl.ds(r, HEADS, stride=R), :] = o
        pr_l[pl.ds(r, HEADS, stride=R), :] = jnp.broadcast_to(lse, (HEADS, D))

    span = ptab_ref.shape[1] * pk.shape[1]
    lane = iota((HEADS, span), 1)
    own = lax.rem(lane, 2) == iota((HEADS, span), 0) // G

    def first_keys():
        loads["tk"].wait()
        sort_keys(tk_raw, k_te, 0, positions // 2, 0)

    def last_keys():
        sort_keys(tk_raw, k_te, positions // 2, positions, 0)

    def own_shared():
        loads["sk"].wait()
        sort_keys(sk_raw.at[0], k_sh, 0, half, 0)
        loads["sv"].wait()
        sort_values(sv_raw.at[0], v_sh, 0, half, 0)

    def first_values():
        loads["tv"].wait()
        sort_values(tv_raw, v_te, 0, positions // 2, 0)

    def last_values():
        sort_values(tv_raw, v_te, positions // 2, positions, 0)

    work = [
        lambda: (mark(0), mark(1)),
        lambda: (mark(2), mark(3)),
        first_keys,
        last_keys,
        own_shared,
        first_values,
        last_values,
    ]
    last = len(groups) - 1
    for turn in range(max(len(work), last + 3)):
        if turn < len(work):
            work[turn]()
        if turn < last:
            z_wait(q_all, qz_s, qz_r, turn + 1)
            forward(*q_line, turn + 1)
        if 1 <= turn <= last + 1:
            relay(*q_line, turn - 1)
    loads["pk"].wait()
    loads["pv"].wait()
    for group in range(len(groups)):
        far_wait(*q_line, group)

    def chunk_queries(xx, kv):
        return q_all[xx, :, kv * COLUMNS:(kv + 1) * COLUMNS, :].reshape(zcols, D)

    for kv in range(KV):
        total = dot(onehot[0], chunk_queries(0, kv))
        for xx in range(1, NX):
            total += dot(onehot[xx], chunk_queries(xx, kv))
        qt_send[kv] = total.astype(BF16)
    go(qt_send, qt_recv, pair_s.at[2], pair_r.at[2], pair)

    arrived(sk_raw.at[1], pair_s.at[0], pair_r.at[0])
    sort_keys(sk_raw.at[1], k_sh, 0, half, half)
    arrived(sv_raw.at[1], pair_s.at[1], pair_r.at[1])
    sort_values(sv_raw.at[1], v_sh, 0, half, half)

    width = min(256, zcols)

    def shared(xx):
        for kv in range(KV):
            for c in range(0, zcols, width):
                zs = slice(c // COLUMNS, (c + width) // COLUMNS)
                queries = q_all[xx, zs, kv * COLUMNS:(kv + 1) * COLUMNS, :].reshape(width, D)
                s = dot_t(k_sh[kv], queries)
                m = jnp.max(s, axis=0, keepdims=True)
                p = jnp.exp2((s - m) * SCALE)
                l = jnp.sum(p, axis=0, keepdims=True)
                sh_o[xx, kv, :, c:c + width] = dot(v_sh[kv], p.astype(BF16)) / l
                lse = m * SCALE + jnp.log2(l)
                sh_l[xx, kv, :, c:c + width] = jnp.broadcast_to(lse, (8, width))

    for r in range(R // 2):
        private(r)
    shared(3)

    arrived(qt_recv, pair_s.at[2], pair_r.at[2])
    extent = tlen_ref[tenant] - lax.rem(seq, 4) * positions
    step_size = min(1024, positions)
    for kv in range(KV):
        queries = (qt_send[kv].astype(F32) + qt_recv[kv].astype(F32)).astype(BF16)
        te_m[...] = jnp.full(te_m.shape, DEAD, F32)
        te_l[...] = jnp.zeros(te_l.shape, F32)
        te_acc[...] = jnp.zeros(te_acc.shape, F32)

        def step(i, carry):
            base = pl.multiple_of(i * step_size, step_size)
            s = dot_t(k_te[kv, pl.ds(base, step_size), :], queries)
            s = jnp.where(iota((step_size, SLOTS), 0) < extent - base, s, DEAD)
            m_old = te_m[:1]
            m = jnp.maximum(m_old, jnp.max(s, axis=0, keepdims=True))
            p = jnp.exp2((s - m) * SCALE)
            keep = jnp.exp2((m_old - m) * SCALE)
            te_m[:1] = m
            te_l[:1] = te_l[:1] * keep + jnp.sum(p, axis=0, keepdims=True)
            te_acc[...] = te_acc[...] * keep + dot(v_te[kv, :, pl.ds(base, step_size)], p.astype(BF16))
            return carry

        lax.fori_loop(0, positions // step_size, step, 0)
        l = te_l[:1]
        to_send[kv] = (te_acc[...] / l).astype(BF16)
        lse = jnp.where(extent > 0, te_m[:1] * SCALE + jnp.log2(l), DEAD)
        tl_send[kv] = jnp.broadcast_to(lse, (8, SLOTS))
    go(to_send, to_recv, pair_s.at[3], pair_r.at[3], pair)
    go(tl_send, tl_recv, pair_s.at[4], pair_r.at[4], pair)
    go(w_hbm, w.at[1], pair_s.at[5], pair_r.at[5], pair)

    def tenants():
        arrived(to_recv, pair_s.at[3], pair_r.at[3])
        arrived(tl_recv, pair_s.at[4], pair_r.at[4])
        for kv in range(KV):
            l1, l2 = tl_send[kv][:1], tl_recv[kv][:1]
            top = jnp.maximum(l1, l2)
            w1, w2 = jnp.exp2(l1 - top), jnp.exp2(l2 - top)
            whole = w1 + w2
            o = to_send[kv].astype(F32) * (w1 / whole) + to_recv[kv].astype(F32) * (w2 / whole)
            hi = o.astype(BF16)
            te_hi[kv] = hi
            te_lo[kv] = (o - hi.astype(F32)).astype(BF16)
            te_stat[kv] = split3(top + jnp.log2(whole))

    near = zcols // 2

    def merge(slot, extra=None):
        for kv in range(KV):
            for side in range(2):
                cut = slice(side * near, (side + 1) * near)
                spread = onehot[slot, :, cut]
                lse = join3(dot(te_stat[kv], spread))
                lse = jnp.where(keys[slot, :1, cut] >= 0.0, lse, DEAD)
                pieces = [
                    (sh_l[slot, kv, :1, cut], lambda: sh_o[slot, kv, :, cut]),
                    (lse, lambda: dot(te_hi[kv], spread) + dot(te_lo[kv], spread)),
                ]
                if extra == side:
                    pieces.append((join3(xo_half[side, kv, D:, :]), lambda: xo_half[side, kv, :D, :]))
                o, lse = combine(pieces)
                if slot == 0:
                    sh_o[0, kv, :, cut] = o
                    sh_l[0, kv, :, cut] = jnp.broadcast_to(lse, (8, near))
                else:
                    xo_send[slot - 1, kv, :D, cut] = o.astype(BF16)
                    xo_send[slot - 1, kv, D:, cut] = split3(lse)

    for r in range(R // 2, R):
        private(r)
    shared(1)
    shared(2)
    tenants()
    merge(3)
    go(xo_send.at[2, :, :, pl.ds(0, near)], xo_half.at[0], xo_s.at[0], xo_r.at[0], right)
    go(xo_send.at[2, :, :, pl.ds(near, near)], xo_half.at[1], xo_s.at[1], xo_r.at[1], left)
    shared(0)
    merge(0)
    arrived(xo_half.at[0], xo_s.at[0], xo_r.at[0])
    merge(1, 0)
    go(xo_send.at[0], xo_full.at[0], xo_s.at[2], xo_r.at[2], right)
    arrived(xo_half.at[1], xo_s.at[1], xo_r.at[1])
    merge(2, 1)
    go(xo_send.at[1], xo_full.at[1], xo_s.at[3], xo_r.at[3], left)
    arrived(xo_full.at[0], xo_s.at[2], xo_r.at[2])
    arrived(xo_full.at[1], xo_s.at[3], xo_r.at[3])

    both = 2 * COLUMNS
    low = iota((D, both), 1) < COLUMNS
    for c in range(0, zcols, both):
        cut = slice(c, c + both)
        halves, marks = [], []
        for kv in range(KV):
            pieces = [(sh_l[0, kv, :1, cut], lambda: sh_o[0, kv, :, cut])]
            for side in range(2):
                pieces.append((
                    join3(xo_full[side, kv, D:, cut]),
                    lambda side=side: xo_full[side, kv, :D, cut],
                ))
            o, lse = combine(pieces)
            halves.append(o)
            marks.append(jnp.broadcast_to(lse, (8, both)))
        first_o = jnp.where(low, halves[0], pltpu.roll(halves[1], COLUMNS, 1))
        first_l = jnp.where(low[:8], marks[0], pltpu.roll(marks[1], COLUMNS, 1))
        second_o = jnp.where(low, pltpu.roll(halves[0], COLUMNS, 1), halves[1])
        second_l = jnp.where(low[:8], pltpu.roll(marks[0], COLUMNS, 1), marks[1])
        for p, o, lse in ((c // COLUMNS, first_o, first_l), (c // COLUMNS + 1, second_o, second_l)):
            if p == 0:
                zo_own[...] = o
                zl_own[...] = lse
            else:
                q = back(p)
                zo_send[p - 1, :D] = o.astype(BF16)
                zo_send[p - 1, D:] = split3(lse[:1])
                to = device(z_of(zorder[p]), x, b, h)
                go(zo_send.at[p - 1], zo_recv.at[q - 1], zo_s.at[p - 1], zo_r.at[q - 1], to)

    private_o = pr_o[...].T
    private_l = pr_l[...].T[:1]
    pieces = [(private_l, lambda: private_o), (zl_own[:1], lambda: zo_own[...])]
    for p in range(1, NZ):
        arrived(zo_recv.at[p - 1], zo_s.at[p - 1], zo_r.at[p - 1])
        pieces.append((join3(zo_recv[p - 1, D:]), lambda p=p: zo_recv[p - 1, :D]))
    attended, _ = combine(pieces)
    at[0, 0] = attended.T.astype(BF16)

    at_line = (at, ax_s, ax_r)
    z_start(at, az_s, az_r)
    forward(*at_line, 0)
    for group in range(1, len(groups)):
        z_wait(at, az_s, az_r, group)
        forward(*at_line, group)
        relay(*at_line, group - 1)
    relay(*at_line, len(groups) - 1)

    def project(slot):
        wide = at[slot].astype(F32)
        rows = [
            wide[:, i * R:(i + 1) * R, :].reshape(NZ * R, D).astype(BF16) for i in range(HEADS)
        ]
        rows = jnp.concatenate(rows, axis=1)
        for db in range(2):
            sums = dot(rows, w[db])
            for p in range(NZ):
                part[db, z_of(zorder[p]), x_of(xorder[slot])] = sums[p * R:(p + 1) * R]

    loads["w"].wait()
    arrived(w.at[1], pair_s.at[5], pair_r.at[5])
    for slot in range(3):
        project(slot)
    for group in range(len(groups)):
        far_wait(*at_line, group)
    project(3)

    for k in range(1, 2 * NH):
        dh, db = k // 2, k % 2
        src = part.at[db, pl.ds(h_of(dh) * zper, zper)]
        go(src, rs_recv.at[k - 1], rs_s.at[k - 1], rs_r.at[k - 1], device(z, x, b_of(db), h_of(dh)))
    totals = [part[0, pl.ds(h * zper, zper)], None]
    for k in range(1, 2 * NH):
        arrived(rs_recv.at[k - 1], rs_s.at[k - 1], rs_r.at[k - 1])
        got = rs_recv[k - 1]
        totals[k % 2] = got if totals[k % 2] is None else totals[k % 2] + got
    first = jnp.where(b == 0, totals[0], totals[1])
    second = jnp.where(b == 0, totals[1], totals[0])
    rows = jnp.concatenate([first[:, :, None], second[:, :, None]], axis=2)
    out_ref[...] = rows.reshape(zper * NX * 2 * R, D).astype(BF16)

    for copy in started:
        copy.wait_send()


def local(NZ, NX, NH, queries, sk, sv, tk, tv, ids, tlen, plen, ptab, pk, pv, w):
    flat = lambda rows: rows.reshape(rows.shape[0] * KV, D)
    paged = lambda rows: rows.reshape(rows.shape[0], rows.shape[1] * KV, D)
    sk, sv, tk, tv = flat(sk), flat(sv), flat(tk), flat(tv)
    pk, pv = paged(pk), paged(pv)
    shared2, positions = sk.shape[0], tk.shape[0] // KV
    zcols = NZ * COLUMNS
    zper = NZ // NH
    dma = pltpu.SemaphoreType.DMA
    v = pltpu.VMEM
    scratch = [
        v(queries.shape, BF16), v((R * HEADS, D), F32),
        v((2, shared2, D), BF16), v((2, shared2, D), BF16), v(tk.shape, BF16), v(tv.shape, BF16),
        v(pk.shape, BF16), v(pv.shape, BF16), v((2,) + w.shape, BF16),
        v((KV, shared2, D), BF16), v((KV, D, shared2), BF16),
        v((KV, positions, D), BF16), v((KV, D, positions), BF16),
        v((NX, NZ, R * HEADS, D), BF16), v((NX, SLOTS, zcols), BF16), v((NX, 8, zcols), F32),
        v((KV, SLOTS, D), BF16), v((KV, SLOTS, D), BF16),
        v((8, SLOTS), F32), v((8, SLOTS), F32), v((D, SLOTS), F32),
        v((KV, D, SLOTS), BF16), v((KV, D, SLOTS), BF16),
        v((KV, 8, SLOTS), F32), v((KV, 8, SLOTS), F32),
        v((KV, D, SLOTS), BF16), v((KV, D, SLOTS), BF16), v((KV, 16, SLOTS), BF16),
        v((NX, KV, D, zcols), F32), v((NX, KV, 8, zcols), F32),
        v((3, KV, D + STAT, zcols), BF16), v((2, KV, D + STAT, zcols // 2), BF16),
        v((2, KV, D + STAT, zcols), BF16),
        v((D, R * HEADS), F32), v((8, R * HEADS), F32),
        v((NZ - 1, D + STAT, R * HEADS), BF16), v((NZ - 1, D + STAT, R * HEADS), BF16),
        v((R * HEADS, D), F32), v((R * HEADS, D), F32),
        v((NX, NZ, R * HEADS, D), BF16), v((2, NZ, NX, R, D), F32),
        v((2 * NH - 1, zper, NX, R, D), F32),
        dma((8,)),
    ]
    lines = 16
    for count in (NZ - 1, lines, 6, 4, NZ - 1, NZ - 1, lines, 2 * NH - 1):
        scratch += [dma((count,)), dma((count,))]
    hbm = pl.BlockSpec(memory_space=pl.ANY)
    smem = pl.BlockSpec(memory_space=pltpu.SMEM)
    vmem = pl.BlockSpec(memory_space=pltpu.VMEM)
    return pl.pallas_call(
        functools.partial(kernel, NZ, NX, NH),
        out_shape=jax.ShapeDtypeStruct((zper * NX * 2 * R, D), BF16),
        in_specs=[hbm] * 5 + [vmem, smem, smem, smem] + [hbm] * 3,
        out_specs=vmem,
        scratch_shapes=scratch,
        compiler_params=pltpu.CompilerParams(
            collective_id=0, has_side_effects=True, vmem_limit_bytes=56 * 1024 * 1024
        ),
    )(queries, sk, sv, tk, tv, ids.reshape(1, -1), tlen, plen, ptab, pk, pv, w)


def solution(mesh):
    sizes = dict(mesh.shape)
    NX = 4
    NZ = sizes["seq"] // (2 * NX)
    placed = (
        P("seq", "head", None),
        P("seq", "head", None),
        P("seq", "head", None),
        P("seq", "head", None),
        P("seq", "head", None),
        P(),
        P(),
        P("seq"),
        P("seq", None),
        P("seq", None, "head", None),
        P("seq", None, "head", None),
        P("head", "seq"),
    )
    return jax.shard_map(
        functools.partial(local, NZ, NX, sizes["head"]),
        mesh=mesh, in_specs=placed, out_specs=P("head", "seq"), check_vma=False,
    )
```

time: 102 us -> 97.8 us (0.959)
  Pallas kernels: 99.9 us -> 96.2 us
    pallas_call x1, Pallas kernels: 99.9 us -> 96.2 us  [local(): pl.pallas_call(functools.partial(kernel, NZ, NX, NH), out_shape=jax.Shape...]
where the time goes in v2:
time: 97.8 us; the launch traced here: 97.6 us
  Pallas kernels  96.2 us (98%)
  local copies, waits for them, and re-layouts  1.38 us (1%)
    pallas_call x1, Pallas kernels, local(): pl.pallas_call(functools.partial(kernel, NZ, NX, NH), out_shape=jax.Shape...  96.2 us

profile of v2, /device:TPU:1, one launch (start us, length us, event | category | flops | bytes accessed | tf_op | source)
XLA Modules:
  0.0 97.6 jit_solution(15187888546053002580)
XLA Ops:
  0.0 96.2 %shard_map.118 = bf16[128,128]{1,0:T(8,128)(2,1)} custom-call(bf16[8,16,128]{2,1,0:T(8,128)(2,1)} %q_hbm.1, bf16[1024,128]{1,0:T(8,128)(2,1)} %bitcast.11, bf16[1024,128]{1,0:T(8,128)(2,1)} %bitcast.12, bf16[8192,128]{1,0:T(8,128)(2,1)} %bitcast.9, bf16[8192,128]{1,0:T(8,128)(2,1)} %bitcast.10, s32[1,512]{1,0:T(1,128)} %bitcast.13, s32[16]{0:T(128)} %tlen_ref.1, ...), custom_call_target="tpu_custom_call" | custom-call | tf_op jit(solution)/shard_map/pallas_call | solution.py:560
  96.2 1.4 %copy.14 = bf16[128,128]{1,0:T(8,128)(2,1)} copy(bf16[128,128]{1,0:T(8,128)(2,1)} %shard_map.118) | data formatting | bytes 65536

commit v3 on v2

--- a/solution.py
+++ b/solution.py
@@ -73,13 +73,13 @@
     q_raw, q_wide, sk_raw, sv_raw, tk_raw, tv_raw, pk, pv, w,
     k_sh, v_sh, k_te, v_te,
     q_all, onehot, keys, qt_send, qt_recv,
-    te_m, te_l, te_acc, to_send, to_recv, tl_send, tl_recv,
+    te_m, te_l, te_acc, te_own, te_lse, to_send, to_recv,
     te_hi, te_lo, te_stat, sh_o, sh_l,
     xo_send, xo_half, xo_full, zo_own, zl_own, zo_send, zo_recv,
-    pr_o, pr_l, at, part, rs_recv,
+    pr_o, pr_l, at, part, rs_recv, fx_send, final,
     in_sem,
     qz_s, qz_r, qx_s, qx_r, pair_s, pair_r, xo_s, xo_r,
-    zo_s, zo_r, az_s, az_r, ax_s, ax_r, rs_s, rs_r,
+    zo_s, zo_r, az_s, az_r, wx_s, wx_r, rs_s, rs_r, fx_s, fx_r,
 ):
     seq = lax.axis_index("seq")
     h = lax.axis_index("head")
@@ -98,7 +98,7 @@
 
     zorder = [(p + 1) // 2 if p % 2 else -(p // 2) for p in range(NZ)]
     xorder = [0, 1, -1, 2]
-    cuts = [0, 1, 3, 5, 8] if NZ == 8 else [0, 1, NZ]
+    cuts = [0, 1, 5, 8] if NZ == 8 else [0, 1, NZ]
     groups = list(zip(cuts[:-1], cuts[1:]))
 
     def back(p):
@@ -142,7 +142,7 @@
         ("tv", tv_hbm, tv_raw),
         ("pk", pk_hbm, pk),
         ("pv", pv_hbm, pv),
-        ("w", w_hbm, w.at[0]),
+        ("w", w_hbm, w.at[0, 0]),
     )):
         loads[name] = pltpu.make_async_copy(src, dst, in_sem.at[at_sem])
         loads[name].start()
@@ -164,7 +164,7 @@
 
     pl.semaphore_wait(barrier, len(peers))
 
-    left, right = device(z, x_of(-1), b, h), device(z, x_of(1), b, h)
+    left, right, far = device(z, x_of(-1), b, h), device(z, x_of(1), b, h), device(z, x_of(2), b, h)
 
     def z_start(buf, zs, zr):
         for p in range(1, NZ):
@@ -176,34 +176,25 @@
             if p > 0:
                 arrived(buf.at[0, p], zs.at[p - 1], zr.at[p - 1])
 
-    def block(buf, slot, group, kind=None):
+    def block(slot, group):
         first, last = groups[group]
-        if kind is None:
-            return buf.at[slot, pl.ds(first, last - first)]
-        return buf.at[slot, pl.ds(first, last - first), pl.ds((kind - 2) * COLUMNS, COLUMNS)]
-
-    def forward(buf, xs, xr, group):
-        k = 4 * group
-        go(block(buf, 0, group), block(buf, 2, group), xs.at[k], xr.at[k], right)
-        go(block(buf, 0, group), block(buf, 1, group), xs.at[k + 1], xr.at[k + 1], left)
-
-    def relay(buf, xs, xr, group):
-        k = 4 * group
-        arrived(block(buf, 2, group), xs.at[k], xr.at[k])
-        go(block(buf, 2, group, 2), block(buf, 3, group, 2), xs.at[k + 2], xr.at[k + 2], right)
-        arrived(block(buf, 1, group), xs.at[k + 1], xr.at[k + 1])
-        go(block(buf, 1, group, 3), block(buf, 3, group, 3), xs.at[k + 3], xr.at[k + 3], left)
-
-    def far_wait(buf, xs, xr, group):
-        for kind in (2, 3):
-            k = 4 * group + kind
-            arrived(block(buf, 3, group, kind), xs.at[k], xr.at[k])
-
-    q_line = (q_all, qx_s, qx_r)
+        return q_all.at[slot, pl.ds(first, last - first)]
+
+    def forward(group):
+        for slot, to in ((2, right), (1, left), (3, far)):
+            k = 3 * group + slot - 1
+            go(block(0, group), block(slot, group), qx_s.at[k], qx_r.at[k], to)
+
+    def x_wait(slot):
+        for group in range(len(groups)):
+            k = 3 * group + slot - 1
+            arrived(block(slot, group), qx_s.at[k], qx_r.at[k])
+
     z_start(q_all, qz_s, qz_r)
-    forward(*q_line, 0)
+    forward(0)
     go(sk_hbm, sk_raw.at[1], pair_s.at[0], pair_r.at[0], pair)
     go(sv_hbm, sv_raw.at[1], pair_s.at[1], pair_r.at[1], pair)
+    go(w_hbm, w.at[0, 1], pair_s.at[2], pair_r.at[2], pair)
 
     row, col = iota((2 * D, 2 * D), 0), iota((2 * D, 2 * D), 1)
     sort = (col == jnp.where(row < D, 2 * row, 2 * (row - D) + 1)).astype(F32).astype(BF16)
@@ -290,43 +281,11 @@
     def last_values():
         sort_values(tv_raw, v_te, positions // 2, positions, 0)
 
-    work = [
-        lambda: (mark(0), mark(1)),
-        lambda: (mark(2), mark(3)),
-        first_keys,
-        last_keys,
-        own_shared,
-        first_values,
-        last_values,
-    ]
-    last = len(groups) - 1
-    for turn in range(max(len(work), last + 3)):
-        if turn < len(work):
-            work[turn]()
-        if turn < last:
-            z_wait(q_all, qz_s, qz_r, turn + 1)
-            forward(*q_line, turn + 1)
-        if 1 <= turn <= last + 1:
-            relay(*q_line, turn - 1)
-    loads["pk"].wait()
-    loads["pv"].wait()
-    for group in range(len(groups)):
-        far_wait(*q_line, group)
-
-    def chunk_queries(xx, kv):
-        return q_all[xx, :, kv * COLUMNS:(kv + 1) * COLUMNS, :].reshape(zcols, D)
-
-    for kv in range(KV):
-        total = dot(onehot[0], chunk_queries(0, kv))
-        for xx in range(1, NX):
-            total += dot(onehot[xx], chunk_queries(xx, kv))
-        qt_send[kv] = total.astype(BF16)
-    go(qt_send, qt_recv, pair_s.at[2], pair_r.at[2], pair)
-
-    arrived(sk_raw.at[1], pair_s.at[0], pair_r.at[0])
-    sort_keys(sk_raw.at[1], k_sh, 0, half, half)
-    arrived(sv_raw.at[1], pair_s.at[1], pair_r.at[1])
-    sort_values(sv_raw.at[1], v_sh, 0, half, half)
+    def pair_shared():
+        arrived(sk_raw.at[1], pair_s.at[0], pair_r.at[0])
+        sort_keys(sk_raw.at[1], k_sh, 0, half, half)
+        arrived(sv_raw.at[1], pair_s.at[1], pair_r.at[1])
+        sort_values(sv_raw.at[1], v_sh, 0, half, half)
 
     width = min(256, zcols)
 
@@ -343,14 +302,51 @@
                 lse = m * SCALE + jnp.log2(l)
                 sh_l[xx, kv, :, c:c + width] = jnp.broadcast_to(lse, (8, width))
 
-    for r in range(R // 2):
+    mark(0)
+    mark(1)
+    z_wait(q_all, qz_s, qz_r, 1)
+    forward(1)
+    mark(2)
+    mark(3)
+    for group in range(2, len(groups)):
+        z_wait(q_all, qz_s, qz_r, group)
+        forward(group)
+    first_keys()
+    last_keys()
+    own_shared()
+    loads["pk"].wait()
+    loads["pv"].wait()
+    for r in range(R):
         private(r)
-    shared(3)
-
-    arrived(qt_recv, pair_s.at[2], pair_r.at[2])
+    pair_shared()
+    shared(0)
+    first_values()
+    for slot_at in (2, 1, 3):
+        x_wait(slot_at)
+
+    def chunk_queries(xx, kv):
+        return q_all[xx, :, kv * COLUMNS:(kv + 1) * COLUMNS, :].reshape(zcols, D)
+
+    for kv in range(KV):
+        total = dot(onehot[0], chunk_queries(0, kv))
+        for xx in range(1, NX):
+            total += dot(onehot[xx], chunk_queries(xx, kv))
+        qt_send[kv] = total.astype(BF16)
+        go(qt_send.at[kv], qt_recv.at[kv], pair_s.at[3 + kv], pair_r.at[3 + kv], pair)
+
+    last_values()
+    loads["w"].wait()
+    arrived(w.at[0, 1], pair_s.at[2], pair_r.at[2])
+    go(w.at[0], w.at[2], wx_s.at[0], wx_r.at[0], right)
+    go(w.at[0], w.at[1], wx_s.at[1], wx_r.at[1], left)
+    shared(1)
+    shared(2)
+
     extent = tlen_ref[tenant] - lax.rem(seq, 4) * positions
     step_size = min(1024, positions)
-    for kv in range(KV):
+
+    def tenant_part(kv):
+        arrived(qt_recv.at[kv], pair_s.at[3 + kv], pair_r.at[3 + kv])
         queries = (qt_send[kv].astype(F32) + qt_recv[kv].astype(F32)).astype(BF16)
         te_m[...] = jnp.full(te_m.shape, DEAD, F32)
         te_l[...] = jnp.zeros(te_l.shape, F32)
@@ -371,68 +367,72 @@
 
         lax.fori_loop(0, positions // step_size, step, 0)
         l = te_l[:1]
-        to_send[kv] = (te_acc[...] / l).astype(BF16)
+        o = te_acc[...] * (1.0 / l)
         lse = jnp.where(extent > 0, te_m[:1] * SCALE + jnp.log2(l), DEAD)
-        tl_send[kv] = jnp.broadcast_to(lse, (8, SLOTS))
-    go(to_send, to_recv, pair_s.at[3], pair_r.at[3], pair)
-    go(tl_send, tl_recv, pair_s.at[4], pair_r.at[4], pair)
-    go(w_hbm, w.at[1], pair_s.at[5], pair_r.at[5], pair)
-
-    def tenants():
-        arrived(to_recv, pair_s.at[3], pair_r.at[3])
-        arrived(tl_recv, pair_s.at[4], pair_r.at[4])
-        for kv in range(KV):
-            l1, l2 = tl_send[kv][:1], tl_recv[kv][:1]
-            top = jnp.maximum(l1, l2)
-            w1, w2 = jnp.exp2(l1 - top), jnp.exp2(l2 - top)
-            whole = w1 + w2
-            o = to_send[kv].astype(F32) * (w1 / whole) + to_recv[kv].astype(F32) * (w2 / whole)
-            hi = o.astype(BF16)
-            te_hi[kv] = hi
-            te_lo[kv] = (o - hi.astype(F32)).astype(BF16)
-            te_stat[kv] = split3(top + jnp.log2(whole))
+        te_own[kv] = o
+        te_lse[kv] = jnp.broadcast_to(lse, (8, SLOTS))
+        to_send[kv, :D] = o.astype(BF16)
+        to_send[kv, D:] = split3(lse)
+        go(to_send.at[kv], to_recv.at[kv], pair_s.at[5 + kv], pair_r.at[5 + kv], pair)
+
+    def tenants(kv):
+        arrived(to_recv.at[kv], pair_s.at[5 + kv], pair_r.at[5 + kv])
+        o, lse = combine([
+            (te_lse[kv, :1], lambda: te_own[kv]),
+            (join3(to_recv[kv, D:]), lambda: to_recv[kv, :D]),
+        ])
+        hi = o.astype(BF16)
+        te_hi[kv] = hi
+        te_lo[kv] = (o - hi.astype(F32)).astype(BF16)
+        te_stat[kv] = split3(lse)
+
+    tenant_part(0)
+    tenant_part(1)
+    shared(3)
 
     near = zcols // 2
 
-    def merge(slot, extra=None):
-        for kv in range(KV):
-            for side in range(2):
-                cut = slice(side * near, (side + 1) * near)
-                spread = onehot[slot, :, cut]
-                lse = join3(dot(te_stat[kv], spread))
-                lse = jnp.where(keys[slot, :1, cut] >= 0.0, lse, DEAD)
-                pieces = [
-                    (sh_l[slot, kv, :1, cut], lambda: sh_o[slot, kv, :, cut]),
-                    (lse, lambda: dot(te_hi[kv], spread) + dot(te_lo[kv], spread)),
-                ]
-                if extra == side:
-                    pieces.append((join3(xo_half[side, kv, D:, :]), lambda: xo_half[side, kv, :D, :]))
-                o, lse = combine(pieces)
-                if slot == 0:
-                    sh_o[0, kv, :, cut] = o
-                    sh_l[0, kv, :, cut] = jnp.broadcast_to(lse, (8, near))
-                else:
-                    xo_send[slot - 1, kv, :D, cut] = o.astype(BF16)
-                    xo_send[slot - 1, kv, D:, cut] = split3(lse)
-
-    for r in range(R // 2, R):
-        private(r)
-    shared(1)
-    shared(2)
-    tenants()
-    merge(3)
-    go(xo_send.at[2, :, :, pl.ds(0, near)], xo_half.at[0], xo_s.at[0], xo_r.at[0], right)
-    go(xo_send.at[2, :, :, pl.ds(near, near)], xo_half.at[1], xo_s.at[1], xo_r.at[1], left)
-    shared(0)
-    merge(0)
-    arrived(xo_half.at[0], xo_s.at[0], xo_r.at[0])
-    merge(1, 0)
-    go(xo_send.at[0], xo_full.at[0], xo_s.at[2], xo_r.at[2], right)
-    arrived(xo_half.at[1], xo_s.at[1], xo_r.at[1])
-    merge(2, 1)
-    go(xo_send.at[1], xo_full.at[1], xo_s.at[3], xo_r.at[3], left)
-    arrived(xo_full.at[0], xo_s.at[2], xo_r.at[2])
-    arrived(xo_full.at[1], xo_s.at[3], xo_r.at[3])
+    def merge(slot, kv, extra=None):
+        for side in range(2):
+            cut = slice(side * near, (side + 1) * near)
+            spread = onehot[slot, :, cut]
+            lse = join3(dot(te_stat[kv], spread))
+            lse = jnp.where(keys[slot, :1, cut] >= 0.0, lse, DEAD)
+            pieces = [
+                (sh_l[slot, kv, :1, cut], lambda: sh_o[slot, kv, :, cut]),
+                (lse, lambda: dot(te_hi[kv], spread) + dot(te_lo[kv], spread)),
+            ]
+            if extra == side:
+                pieces.append((join3(xo_half[side, kv, D:, :]), lambda: xo_half[side, kv, :D, :]))
+            o, lse = combine(pieces)
+            if slot == 0:
+                sh_o[0, kv, :, cut] = o
+                sh_l[0, kv, :, cut] = jnp.broadcast_to(lse, (8, near))
+            else:
+                xo_send[slot - 1, kv, :D, cut] = o.astype(BF16)
+                xo_send[slot - 1, kv, D:, cut] = split3(lse)
+
+    for kv in range(KV):
+        tenants(kv)
+        merge(3, kv)
+        for side, to in ((0, right), (1, left)):
+            k = 4 * kv + side
+            half_cut = pl.ds(side * near, near)
+            go(xo_send.at[2, kv, :, half_cut], xo_half.at[side, kv], xo_s.at[k], xo_r.at[k], to)
+    for kv in range(KV):
+        merge(0, kv)
+    for kv in range(KV):
+        for side, to in ((0, right), (1, left)):
+            k = 4 * kv + side
+            arrived(xo_half.at[side, kv], xo_s.at[k], xo_r.at[k])
+            merge(1 + side, kv, side)
+            go(xo_send.at[side, kv], xo_full.at[side, kv], xo_s.at[k + 2], xo_r.at[k + 2], to)
+    private_o = pr_o[...].T
+    private_l = pr_l[...].T[:1]
+    for kv in range(KV):
+        for side in range(2):
+            k = 4 * kv + side + 2
+            arrived(xo_full.at[side, kv], xo_s.at[k], xo_r.at[k])
 
     both = 2 * COLUMNS
     low = iota((D, both), 1) < COLUMNS
@@ -464,8 +464,11 @@
                 to = device(z_of(zorder[p]), x, b, h)
                 go(zo_send.at[p - 1], zo_recv.at[q - 1], zo_s.at[p - 1], zo_r.at[q - 1], to)
 
-    private_o = pr_o[...].T
-    private_l = pr_l[...].T[:1]
+    arrived(w.at[2], wx_s.at[0], wx_r.at[0])
+    go(w.at[2, 0], w.at[3, 0], wx_s.at[2], wx_r.at[2], right)
+    arrived(w.at[1], wx_s.at[1], wx_r.at[1])
+    go(w.at[1, 1], w.at[3, 1], wx_s.at[3], wx_r.at[3], left)
+
     pieces = [(private_l, lambda: private_o), (zl_own[:1], lambda: zo_own[...])]
     for p in range(1, NZ):
         arrived(zo_recv.at[p - 1], zo_s.at[p - 1], zo_r.at[p - 1])
@@ -473,33 +476,20 @@
     attended, _ = combine(pieces)
     at[0, 0] = attended.T.astype(BF16)
 
-    at_line = (at, ax_s, ax_r)
     z_start(at, az_s, az_r)
-    forward(*at_line, 0)
-    for group in range(1, len(groups)):
+    for group in range(len(groups)):
         z_wait(at, az_s, az_r, group)
-        forward(*at_line, group)
-        relay(*at_line, group - 1)
-    relay(*at_line, len(groups) - 1)
-
-    def project(slot):
-        wide = at[slot].astype(F32)
-        rows = [
-            wide[:, i * R:(i + 1) * R, :].reshape(NZ * R, D).astype(BF16) for i in range(HEADS)
-        ]
-        rows = jnp.concatenate(rows, axis=1)
-        for db in range(2):
-            sums = dot(rows, w[db])
+    wide = at[0].astype(F32)
+    rows = jnp.concatenate([
+        wide[:, i * R:(i + 1) * R, :].reshape(NZ * R, D).astype(BF16) for i in range(HEADS)
+    ], axis=1)
+    arrived(w.at[3, 0], wx_s.at[2], wx_r.at[2])
+    arrived(w.at[3, 1], wx_s.at[3], wx_r.at[3])
+    for db in (1, 0):
+        for slot in range(NX):
+            sums = dot(rows, w[slot, db])
             for p in range(NZ):
-                part[db, z_of(zorder[p]), x_of(xorder[slot])] = sums[p * R:(p + 1) * R]
-
-    loads["w"].wait()
-    arrived(w.at[1], pair_s.at[5], pair_r.at[5])
-    for slot in range(3):
-        project(slot)
-    for group in range(len(groups)):
-        far_wait(*at_line, group)
-    project(3)
+                part[db, z_of(zorder[p]), slot] = sums[p * R:(p + 1) * R]
 
     for k in range(1, 2 * NH):
         dh, db = k // 2, k % 2
@@ -512,8 +502,18 @@
         totals[k % 2] = got if totals[k % 2] is None else totals[k % 2] + got
     first = jnp.where(b == 0, totals[0], totals[1])
     second = jnp.where(b == 0, totals[1], totals[0])
-    rows = jnp.concatenate([first[:, :, None], second[:, :, None]], axis=2)
-    out_ref[...] = rows.reshape(zper * NX * 2 * R, D).astype(BF16)
+
+    for slot, to in ((3, far), (1, right), (2, left), (0, None)):
+        rows = jnp.concatenate([first[:, slot], second[:, slot]], axis=1).astype(BF16)
+        if to is None:
+            final[:, x] = rows
+        else:
+            fx_send[slot - 1] = rows
+            k = slot - 1
+            go(fx_send.at[k], final.at[:, x], fx_s.at[k], fx_r.at[k], to)
+    for slot, offset in ((3, 2), (1, -1), (2, 1)):
+        arrived(final.at[:, x_of(offset)], fx_s.at[slot - 1], fx_r.at[slot - 1])
+    out_ref[...] = final[...].reshape(zper * NX * 2 * R, D)
 
     for copy in started:
         copy.wait_send()
@@ -532,14 +532,14 @@
     scratch = [
         v(queries.shape, BF16), v((R * HEADS, D), F32),
         v((2, shared2, D), BF16), v((2, shared2, D), BF16), v(tk.shape, BF16), v(tv.shape, BF16),
-        v(pk.shape, BF16), v(pv.shape, BF16), v((2,) + w.shape, BF16),
+        v(pk.shape, BF16), v(pv.shape, BF16), v((NX, 2) + w.shape, BF16),
         v((KV, shared2, D), BF16), v((KV, D, shared2), BF16),
         v((KV, positions, D), BF16), v((KV, D, positions), BF16),
         v((NX, NZ, R * HEADS, D), BF16), v((NX, SLOTS, zcols), BF16), v((NX, 8, zcols), F32),
         v((KV, SLOTS, D), BF16), v((KV, SLOTS, D), BF16),
         v((8, SLOTS), F32), v((8, SLOTS), F32), v((D, SLOTS), F32),
-        v((KV, D, SLOTS), BF16), v((KV, D, SLOTS), BF16),
-        v((KV, 8, SLOTS), F32), v((KV, 8, SLOTS), F32),
+        v((KV, D, SLOTS), F32), v((KV, 8, SLOTS), F32),
+        v((KV, D + STAT, SLOTS), BF16), v((KV, D + STAT, SLOTS), BF16),
         v((KV, D, SLOTS), BF16), v((KV, D, SLOTS), BF16), v((KV, 16, SLOTS), BF16),
         v((NX, KV, D, zcols), F32), v((NX, KV, 8, zcols), F32),
         v((3, KV, D + STAT, zcols), BF16), v((2, KV, D + STAT, zcols // 2), BF16),
@@ -547,12 +547,12 @@
         v((D, R * HEADS), F32), v((8, R * HEADS), F32),
         v((NZ - 1, D + STAT, R * HEADS), BF16), v((NZ - 1, D + STAT, R * HEADS), BF16),
         v((R * HEADS, D), F32), v((R * HEADS, D), F32),
-        v((NX, NZ, R * HEADS, D), BF16), v((2, NZ, NX, R, D), F32),
+        v((1, NZ, R * HEADS, D), BF16), v((2, NZ, NX, R, D), F32),
         v((2 * NH - 1, zper, NX, R, D), F32),
+        v((NX - 1, zper, 2 * R, D), BF16), v((zper, NX, 2 * R, D), BF16),
         dma((8,)),
     ]
-    lines = 16
-    for count in (NZ - 1, lines, 6, 4, NZ - 1, NZ - 1, lines, 2 * NH - 1):
+    for count in (NZ - 1, 9, 7, 4 * KV, NZ - 1, NZ - 1, 4, 2 * NH - 1, NX - 1):
         scratch += [dma((count,)), dma((count,))]
     hbm = pl.BlockSpec(memory_space=pl.ANY)
     smem = pl.BlockSpec(memory_space=pltpu.SMEM)

time: 97.8 us -> 100 us (1.022)
  Pallas kernels: 96.2 us -> 98.5 us
    pallas_call x1, Pallas kernels: 96.2 us -> 98.5 us  [local(): pl.pallas_call(functools.partial(kernel, NZ, NX, NH), out_shape=jax.Shape...]
where the time goes in v3:
time: 100 us; the launch traced here: 99.9 us
  Pallas kernels  98.5 us (98%)
  local copies, waits for them, and re-layouts  1.38 us (1%)
    pallas_call x1, Pallas kernels, local(): pl.pallas_call(functools.partial(kernel, NZ, NX, NH), out_shape=jax.Shape...  98.5 us

profile of v3, /device:TPU:1, one launch (start us, length us, event | category | flops | bytes accessed | tf_op | source)
XLA Modules:
  0.0 99.9 jit_solution(1753605616604877141)
XLA Ops:
  0.0 98.5 %shard_map.118 = bf16[128,128]{1,0:T(8,128)(2,1)} custom-call(bf16[8,16,128]{2,1,0:T(8,128)(2,1)} %q_hbm.1, bf16[1024,128]{1,0:T(8,128)(2,1)} %bitcast.11, bf16[1024,128]{1,0:T(8,128)(2,1)} %bitcast.12, bf16[8192,128]{1,0:T(8,128)(2,1)} %bitcast.9, bf16[8192,128]{1,0:T(8,128)(2,1)} %bitcast.10, s32[1,512]{1,0:T(1,128)} %bitcast.13, s32[16]{0:T(128)} %tlen_ref.1, ...), custom_call_target="tpu_custom_call" | custom-call | tf_op jit(solution)/shard_map/pallas_call | solution.py:560
  98.5 1.4 %copy.14 = bf16[128,128]{1,0:T(8,128)(2,1)} copy(bf16[128,128]{1,0:T(8,128)(2,1)} %shard_map.118) | data formatting | bytes 65536

commit v4 on v3

--- a/solution.py
+++ b/solution.py
@@ -73,8 +73,8 @@
     q_raw, q_wide, sk_raw, sv_raw, tk_raw, tv_raw, pk, pv, w,
     k_sh, v_sh, k_te, v_te,
     q_all, onehot, keys, qt_send, qt_recv,
-    te_m, te_l, te_acc, te_own, te_lse, to_send, to_recv,
-    te_hi, te_lo, te_stat, sh_o, sh_l,
+    te_m, te_l, te_own, to_send, to_recv,
+    te_all, sh_o, sh_l,
     xo_send, xo_half, xo_full, zo_own, zl_own, zo_send, zo_recv,
     pr_o, pr_l, at, part, rs_recv, fx_send, final,
     in_sem,
@@ -136,9 +136,9 @@
     loads = {}
     for at_sem, (name, src, dst) in enumerate((
         ("q", q_hbm, q_raw),
-        ("tk", tk_hbm, tk_raw),
         ("sk", sk_hbm, sk_raw.at[0]),
         ("sv", sv_hbm, sv_raw.at[0]),
+        ("tk", tk_hbm, tk_raw),
         ("tv", tv_hbm, tv_raw),
         ("pk", pk_hbm, pk),
         ("pv", pv_hbm, pv),
@@ -192,9 +192,10 @@
 
     z_start(q_all, qz_s, qz_r)
     forward(0)
-    go(sk_hbm, sk_raw.at[1], pair_s.at[0], pair_r.at[0], pair)
-    go(sv_hbm, sv_raw.at[1], pair_s.at[1], pair_r.at[1], pair)
-    go(w_hbm, w.at[0, 1], pair_s.at[2], pair_r.at[2], pair)
+    loads["sk"].wait()
+    go(sk_raw.at[0], sk_raw.at[1], pair_s.at[0], pair_r.at[0], pair)
+    loads["sv"].wait()
+    go(sv_raw.at[0], sv_raw.at[1], pair_s.at[1], pair_r.at[1], pair)
 
     row, col = iota((2 * D, 2 * D), 0), iota((2 * D, 2 * D), 1)
     sort = (col == jnp.where(row < D, 2 * row, 2 * (row - D) + 1)).astype(F32).astype(BF16)
@@ -235,7 +236,8 @@
         j = iota((1, zcols), 1)
         place = j // COLUMNS
         away = jnp.where(place % 2 == 1, (place + 1) // 2, -(place // 2))
-        owner = seq_of(lax.rem(z + away + NZ, NZ), x_of(xorder[xx]), b)
+        aside = (xx + 1) // 2 * (1 - 2 * lax.rem(xx + 1, 2))
+        owner = seq_of(lax.rem(z + away + NZ, NZ), x_of(aside), b)
         request = owner * R + lax.rem(j, R)
         pick = (iota((requests, zcols), 0) == request).astype(F32).astype(BF16)
         found = dot(slot, pick)[:1]
@@ -261,25 +263,17 @@
     lane = iota((HEADS, span), 1)
     own = lax.rem(lane, 2) == iota((HEADS, span), 0) // G
 
-    def first_keys():
+    def all_keys():
         loads["tk"].wait()
-        sort_keys(tk_raw, k_te, 0, positions // 2, 0)
-
-    def last_keys():
-        sort_keys(tk_raw, k_te, positions // 2, positions, 0)
+        sort_keys(tk_raw, k_te, 0, positions, 0)
 
     def own_shared():
-        loads["sk"].wait()
         sort_keys(sk_raw.at[0], k_sh, 0, half, 0)
-        loads["sv"].wait()
         sort_values(sv_raw.at[0], v_sh, 0, half, 0)
 
-    def first_values():
+    def all_values():
         loads["tv"].wait()
-        sort_values(tv_raw, v_te, 0, positions // 2, 0)
-
-    def last_values():
-        sort_values(tv_raw, v_te, positions // 2, positions, 0)
+        sort_values(tv_raw, v_te, 0, positions, 0)
 
     def pair_shared():
         arrived(sk_raw.at[1], pair_s.at[0], pair_r.at[0])
@@ -289,38 +283,47 @@
 
     width = min(256, zcols)
 
-    def shared(xx):
-        for kv in range(KV):
-            for c in range(0, zcols, width):
-                zs = slice(c // COLUMNS, (c + width) // COLUMNS)
-                queries = q_all[xx, zs, kv * COLUMNS:(kv + 1) * COLUMNS, :].reshape(width, D)
-                s = dot_t(k_sh[kv], queries)
-                m = jnp.max(s, axis=0, keepdims=True)
-                p = jnp.exp2((s - m) * SCALE)
-                l = jnp.sum(p, axis=0, keepdims=True)
-                sh_o[xx, kv, :, c:c + width] = dot(v_sh[kv], p.astype(BF16)) / l
-                lse = m * SCALE + jnp.log2(l)
-                sh_l[xx, kv, :, c:c + width] = jnp.broadcast_to(lse, (8, width))
-
-    mark(0)
-    mark(1)
+    def shared(i):
+        slot, c = i // (zcols // width), lax.rem(i, zcols // width)
+        zs = pl.ds(c * (width // COLUMNS), width // COLUMNS)
+        into = pl.ds(pl.multiple_of(c * width, width), width)
+        scores = [
+            dot_t(k_sh[kv], q_all[slot, zs, kv * COLUMNS:(kv + 1) * COLUMNS, :].reshape(width, D))
+            for kv in range(KV)
+        ]
+        for kv, s in enumerate(scores):
+            m = jnp.max(s, axis=0, keepdims=True)
+            p = jnp.exp2((s - m) * SCALE)
+            l = jnp.sum(p, axis=0, keepdims=True)
+            sh_o[slot, kv, :, into] = dot(v_sh[kv], p.astype(BF16)) * (1.0 / l)
+            sh_l[slot, kv, :, into] = jnp.broadcast_to(m * SCALE + jnp.log2(l), (8, width))
+
+    per_slot = zcols // width
+
+    def loop(first, last, body, unroll=1):
+        def step(i, carry):
+            body(i)
+            return carry
+
+        lax.fori_loop(first, last, step, 0, unroll=unroll)
+
+    for slot_at in range(NX):
+        mark(slot_at)
     z_wait(q_all, qz_s, qz_r, 1)
     forward(1)
-    mark(2)
-    mark(3)
+    all_keys()
     for group in range(2, len(groups)):
         z_wait(q_all, qz_s, qz_r, group)
         forward(group)
-    first_keys()
-    last_keys()
+    loads["w"].wait()
+    go(w.at[0, 0], w.at[0, 1], pair_s.at[2], pair_r.at[2], pair)
     own_shared()
+    all_values()
     loads["pk"].wait()
     loads["pv"].wait()
     for r in range(R):
         private(r)
     pair_shared()
-    shared(0)
-    first_values()
     for slot_at in (2, 1, 3):
         x_wait(slot_at)
 
@@ -332,112 +335,107 @@
         for xx in range(1, NX):
             total += dot(onehot[xx], chunk_queries(xx, kv))
         qt_send[kv] = total.astype(BF16)
-        go(qt_send.at[kv], qt_recv.at[kv], pair_s.at[3 + kv], pair_r.at[3 + kv], pair)
-
-    last_values()
-    loads["w"].wait()
-    arrived(w.at[0, 1], pair_s.at[2], pair_r.at[2])
-    go(w.at[0], w.at[2], wx_s.at[0], wx_r.at[0], right)
-    go(w.at[0], w.at[1], wx_s.at[1], wx_r.at[1], left)
-    shared(1)
-    shared(2)
+
+    go(qt_send, qt_recv, pair_s.at[3], pair_r.at[3], pair)
+
+    go(w.at[0, 0], w.at[2, 0], wx_s.at[0], wx_r.at[0], right)
+    go(w.at[0, 0], w.at[1, 0], wx_s.at[1], wx_r.at[1], left)
+    loop(0, 2 * per_slot, shared)
 
     extent = tlen_ref[tenant] - lax.rem(seq, 4) * positions
     step_size = min(1024, positions)
 
-    def tenant_part(kv):
-        arrived(qt_recv.at[kv], pair_s.at[3 + kv], pair_r.at[3 + kv])
-        queries = (qt_send[kv].astype(F32) + qt_recv[kv].astype(F32)).astype(BF16)
-        te_m[...] = jnp.full(te_m.shape, DEAD, F32)
-        te_l[...] = jnp.zeros(te_l.shape, F32)
-        te_acc[...] = jnp.zeros(te_acc.shape, F32)
-
-        def step(i, carry):
-            base = pl.multiple_of(i * step_size, step_size)
-            s = dot_t(k_te[kv, pl.ds(base, step_size), :], queries)
+    arrived(w.at[0, 1], pair_s.at[2], pair_r.at[2])
+    go(w.at[0, 1], w.at[2, 1], wx_s.at[4], wx_r.at[4], right)
+    go(w.at[0, 1], w.at[1, 1], wx_s.at[5], wx_r.at[5], left)
+    arrived(qt_recv, pair_s.at[3], pair_r.at[3])
+    for kv in range(KV):
+        qt_recv[kv] = (qt_send[kv].astype(F32) + qt_recv[kv].astype(F32)).astype(BF16)
+    te_m[...] = jnp.full(te_m.shape, DEAD, F32)
+    te_l[...] = jnp.zeros(te_l.shape, F32)
+    te_own[...] = jnp.zeros(te_own.shape, F32)
+
+    def tenant_step(i):
+        base = pl.multiple_of(i * step_size, step_size)
+        scores = [dot_t(k_te[kv, pl.ds(base, step_size), :], qt_recv[kv]) for kv in range(KV)]
+        for kv, s in enumerate(scores):
             s = jnp.where(iota((step_size, SLOTS), 0) < extent - base, s, DEAD)
-            m_old = te_m[:1]
+            m_old = te_m[kv, :1]
             m = jnp.maximum(m_old, jnp.max(s, axis=0, keepdims=True))
             p = jnp.exp2((s - m) * SCALE)
             keep = jnp.exp2((m_old - m) * SCALE)
-            te_m[:1] = m
-            te_l[:1] = te_l[:1] * keep + jnp.sum(p, axis=0, keepdims=True)
-            te_acc[...] = te_acc[...] * keep + dot(v_te[kv, :, pl.ds(base, step_size)], p.astype(BF16))
-            return carry
-
-        lax.fori_loop(0, positions // step_size, step, 0)
-        l = te_l[:1]
-        o = te_acc[...] * (1.0 / l)
-        lse = jnp.where(extent > 0, te_m[:1] * SCALE + jnp.log2(l), DEAD)
+            te_m[kv, :1] = m
+            te_l[kv, :1] = te_l[kv, :1] * keep + jnp.sum(p, axis=0, keepdims=True)
+            te_own[kv] = te_own[kv] * keep + dot(v_te[kv, :, pl.ds(base, step_size)], p.astype(BF16))
+
+    loop(0, positions // step_size, tenant_step)
+    for kv in range(KV):
+        l = te_l[kv, :1]
+        o = te_own[kv] * (1.0 / l)
+        lse = jnp.where(extent > 0, te_m[kv, :1] * SCALE + jnp.log2(l), DEAD)
         te_own[kv] = o
-        te_lse[kv] = jnp.broadcast_to(lse, (8, SLOTS))
+        te_l[kv, :1] = lse
         to_send[kv, :D] = o.astype(BF16)
         to_send[kv, D:] = split3(lse)
-        go(to_send.at[kv], to_recv.at[kv], pair_s.at[5 + kv], pair_r.at[5 + kv], pair)
-
-    def tenants(kv):
-        arrived(to_recv.at[kv], pair_s.at[5 + kv], pair_r.at[5 + kv])
+    go(to_send, to_recv, pair_s.at[4], pair_r.at[4], pair)
+    loop(2 * per_slot, 4 * per_slot, shared)
+
+    arrived(to_recv, pair_s.at[4], pair_r.at[4])
+    for kv in range(KV):
         o, lse = combine([
-            (te_lse[kv, :1], lambda: te_own[kv]),
+            (te_l[kv, :1], lambda: te_own[kv]),
             (join3(to_recv[kv, D:]), lambda: to_recv[kv, :D]),
         ])
         hi = o.astype(BF16)
-        te_hi[kv] = hi
-        te_lo[kv] = (o - hi.astype(F32)).astype(BF16)
-        te_stat[kv] = split3(lse)
-
-    tenant_part(0)
-    tenant_part(1)
-    shared(3)
+        te_all[kv, :D] = hi
+        te_all[kv, D:2 * D] = (o - hi.astype(F32)).astype(BF16)
+        te_all[kv, 2 * D:] = split3(lse)
 
     near = zcols // 2
 
-    def merge(slot, kv, extra=None):
-        for side in range(2):
-            cut = slice(side * near, (side + 1) * near)
-            spread = onehot[slot, :, cut]
-            lse = join3(dot(te_stat[kv], spread))
-            lse = jnp.where(keys[slot, :1, cut] >= 0.0, lse, DEAD)
+    def merge(slot, side, extra=False):
+        cut = pl.ds(pl.multiple_of(side * near, near), near)
+        spread = onehot[slot, :, cut]
+        here = keys[slot, :1, cut] >= 0.0
+        height = 2 * D + STAT
+        parts = dot(te_all[...].reshape(KV * height, SLOTS), spread)
+        for kv in range(KV):
+            own_part = parts[kv * height:(kv + 1) * height]
+            lse = jnp.where(here, join3(own_part[2 * D:]), DEAD)
             pieces = [
                 (sh_l[slot, kv, :1, cut], lambda: sh_o[slot, kv, :, cut]),
-                (lse, lambda: dot(te_hi[kv], spread) + dot(te_lo[kv], spread)),
+                (lse, lambda: own_part[:D] + own_part[D:2 * D]),
             ]
-            if extra == side:
+            if extra:
                 pieces.append((join3(xo_half[side, kv, D:, :]), lambda: xo_half[side, kv, :D, :]))
             o, lse = combine(pieces)
-            if slot == 0:
+            if isinstance(slot, int) and slot == 0:
                 sh_o[0, kv, :, cut] = o
                 sh_l[0, kv, :, cut] = jnp.broadcast_to(lse, (8, near))
             else:
                 xo_send[slot - 1, kv, :D, cut] = o.astype(BF16)
                 xo_send[slot - 1, kv, D:, cut] = split3(lse)
 
-    for kv in range(KV):
-        tenants(kv)
-        merge(3, kv)
-        for side, to in ((0, right), (1, left)):
-            k = 4 * kv + side
-            half_cut = pl.ds(side * near, near)
-            go(xo_send.at[2, kv, :, half_cut], xo_half.at[side, kv], xo_s.at[k], xo_r.at[k], to)
-    for kv in range(KV):
-        merge(0, kv)
-    for kv in range(KV):
-        for side, to in ((0, right), (1, left)):
-            k = 4 * kv + side
-            arrived(xo_half.at[side, kv], xo_s.at[k], xo_r.at[k])
-            merge(1 + side, kv, side)
-            go(xo_send.at[side, kv], xo_full.at[side, kv], xo_s.at[k + 2], xo_r.at[k + 2], to)
+    for side, to in ((0, right), (1, left)):
+        merge(3, side)
+        half_cut = pl.ds(side * near, near)
+        go(xo_send.at[2, :, :, half_cut], xo_half.at[side], xo_s.at[side], xo_r.at[side], to)
+    loop(0, 2, lambda i: merge(1 + i, 1 - i))
+    loop(0, 2, lambda i: merge(0, i))
+    for side, to in ((0, right), (1, left)):
+        arrived(xo_half.at[side], xo_s.at[side], xo_r.at[side])
+        merge(1 + side, side, True)
+        go(xo_send.at[side], xo_full.at[side], xo_s.at[2 + side], xo_r.at[2 + side], to)
     private_o = pr_o[...].T
     private_l = pr_l[...].T[:1]
-    for kv in range(KV):
-        for side in range(2):
-            k = 4 * kv + side + 2
-            arrived(xo_full.at[side, kv], xo_s.at[k], xo_r.at[k])
+    for side in range(2):
+        arrived(xo_full.at[side], xo_s.at[2 + side], xo_r.at[2 + side])
 
     both = 2 * COLUMNS
     low = iota((D, both), 1) < COLUMNS
-    for c in range(0, zcols, both):
-        cut = slice(c, c + both)
+
+    def join(i):
+        cut = pl.ds(pl.multiple_of(i * both, both), both)
         halves, marks = [], []
         for kv in range(KV):
             pieces = [(sh_l[0, kv, :1, cut], lambda: sh_o[0, kv, :, cut])]
@@ -453,20 +451,24 @@
         first_l = jnp.where(low[:8], marks[0], pltpu.roll(marks[1], COLUMNS, 1))
         second_o = jnp.where(low, pltpu.roll(halves[0], COLUMNS, 1), halves[1])
         second_l = jnp.where(low[:8], pltpu.roll(marks[0], COLUMNS, 1), marks[1])
-        for p, o, lse in ((c // COLUMNS, first_o, first_l), (c // COLUMNS + 1, second_o, second_l)):
-            if p == 0:
-                zo_own[...] = o
-                zl_own[...] = lse
-            else:
-                q = back(p)
-                zo_send[p - 1, :D] = o.astype(BF16)
-                zo_send[p - 1, D:] = split3(lse[:1])
-                to = device(z_of(zorder[p]), x, b, h)
-                go(zo_send.at[p - 1], zo_recv.at[q - 1], zo_s.at[p - 1], zo_r.at[q - 1], to)
-
-    arrived(w.at[2], wx_s.at[0], wx_r.at[0])
+        for p, o, lse in ((2 * i, first_o, first_l), (2 * i + 1, second_o, second_l)):
+            zo_send[p, :D] = o.astype(BF16)
+            zo_send[p, D:] = split3(lse[:1])
+
+        @pl.when(i == 0)
+        def _():
+            zo_own[...] = first_o
+            zl_own[...] = first_l
+
+    loop(0, zcols // both, join, zcols // both)
+    for p in range(1, NZ):
+        q = back(p)
+        to = device(z_of(zorder[p]), x, b, h)
+        go(zo_send.at[p], zo_recv.at[q - 1], zo_s.at[p - 1], zo_r.at[q - 1], to)
+
+    arrived(w.at[2, 0], wx_s.at[0], wx_r.at[0])
     go(w.at[2, 0], w.at[3, 0], wx_s.at[2], wx_r.at[2], right)
-    arrived(w.at[1], wx_s.at[1], wx_r.at[1])
+    arrived(w.at[1, 1], wx_s.at[5], wx_r.at[5])
     go(w.at[1, 1], w.at[3, 1], wx_s.at[3], wx_r.at[3], left)
 
     pieces = [(private_l, lambda: private_o), (zl_own[:1], lambda: zo_own[...])]
@@ -483,13 +485,17 @@
     rows = jnp.concatenate([
         wide[:, i * R:(i + 1) * R, :].reshape(NZ * R, D).astype(BF16) for i in range(HEADS)
     ], axis=1)
+    arrived(w.at[2, 1], wx_s.at[4], wx_r.at[4])
+    arrived(w.at[1, 0], wx_s.at[1], wx_r.at[1])
     arrived(w.at[3, 0], wx_s.at[2], wx_r.at[2])
     arrived(w.at[3, 1], wx_s.at[3], wx_r.at[3])
-    for db in (1, 0):
-        for slot in range(NX):
-            sums = dot(rows, w[slot, db])
+    def project(slot):
+        sums = dot(rows, jnp.concatenate([w[slot, 0], w[slot, 1]], axis=1))
+        for db in range(2):
             for p in range(NZ):
-                part[db, z_of(zorder[p]), slot] = sums[p * R:(p + 1) * R]
+                part[db, z_of(zorder[p]), slot] = sums[p * R:(p + 1) * R, db * D:(db + 1) * D]
+
+    loop(0, NX, project, NX)
 
     for k in range(1, 2 * NH):
         dh, db = k // 2, k % 2
@@ -537,22 +543,21 @@
         v((KV, positions, D), BF16), v((KV, D, positions), BF16),
         v((NX, NZ, R * HEADS, D), BF16), v((NX, SLOTS, zcols), BF16), v((NX, 8, zcols), F32),
         v((KV, SLOTS, D), BF16), v((KV, SLOTS, D), BF16),
-        v((8, SLOTS), F32), v((8, SLOTS), F32), v((D, SLOTS), F32),
-        v((KV, D, SLOTS), F32), v((KV, 8, SLOTS), F32),
+        v((KV, 8, SLOTS), F32), v((KV, 8, SLOTS), F32), v((KV, D, SLOTS), F32),
         v((KV, D + STAT, SLOTS), BF16), v((KV, D + STAT, SLOTS), BF16),
-        v((KV, D, SLOTS), BF16), v((KV, D, SLOTS), BF16), v((KV, 16, SLOTS), BF16),
+        v((KV, 2 * D + STAT, SLOTS), BF16),
         v((NX, KV, D, zcols), F32), v((NX, KV, 8, zcols), F32),
         v((3, KV, D + STAT, zcols), BF16), v((2, KV, D + STAT, zcols // 2), BF16),
         v((2, KV, D + STAT, zcols), BF16),
         v((D, R * HEADS), F32), v((8, R * HEADS), F32),
-        v((NZ - 1, D + STAT, R * HEADS), BF16), v((NZ - 1, D + STAT, R * HEADS), BF16),
+        v((NZ, D + STAT, R * HEADS), BF16), v((NZ - 1, D + STAT, R * HEADS), BF16),
         v((R * HEADS, D), F32), v((R * HEADS, D), F32),
         v((1, NZ, R * HEADS, D), BF16), v((2, NZ, NX, R, D), F32),
         v((2 * NH - 1, zper, NX, R, D), F32),
         v((NX - 1, zper, 2 * R, D), BF16), v((zper, NX, 2 * R, D), BF16),
         dma((8,)),
     ]
-    for count in (NZ - 1, 9, 7, 4 * KV, NZ - 1, NZ - 1, 4, 2 * NH - 1, NX - 1):
+    for count in (NZ - 1, 9, 5, 4, NZ - 1, NZ - 1, 6, 2 * NH - 1, NX - 1):
         scratch += [dma((count,)), dma((count,))]
     hbm = pl.BlockSpec(memory_space=pl.ANY)
     smem = pl.BlockSpec(memory_space=pltpu.SMEM)

time: 100 us -> 94.3 us (0.943)
  Pallas kernels: 98.5 us -> 92.7 us
    pallas_call x1, Pallas kernels: 98.5 us -> 92.7 us  [local(): pl.pallas_call(functools.partial(kernel, NZ, NX, NH), out_shape=jax.Shape...]
where the time goes in v4:
time: 94.3 us; the launch traced here: 94.1 us
  Pallas kernels  92.7 us (98%)
  local copies, waits for them, and re-layouts  1.38 us (1%)
    pallas_call x1, Pallas kernels, local(): pl.pallas_call(functools.partial(kernel, NZ, NX, NH), out_shape=jax.Shape...  92.7 us

profile of v4, /device:TPU:1, one launch (start us, length us, event | category | flops | bytes accessed | tf_op | source)
XLA Modules:
  0.0 94.1 jit_solution(17398801634473030542)
XLA Ops:
  0.0 92.7 %shard_map.118 = bf16[128,128]{1,0:T(8,128)(2,1)} custom-call(bf16[8,16,128]{2,1,0:T(8,128)(2,1)} %q_hbm.1, bf16[1024,128]{1,0:T(8,128)(2,1)} %bitcast.11, bf16[1024,128]{1,0:T(8,128)(2,1)} %bitcast.12, bf16[8192,128]{1,0:T(8,128)(2,1)} %bitcast.9, bf16[8192,128]{1,0:T(8,128)(2,1)} %bitcast.10, s32[1,512]{1,0:T(1,128)} %bitcast.13, s32[16]{0:T(128)} %tlen_ref.1, ...), custom_call_target="tpu_custom_call" | custom-call | tf_op jit(solution)/shard_map/pallas_call | solution.py:565
  92.7 1.4 %copy.14 = bf16[128,128]{1,0:T(8,128)(2,1)} copy(bf16[128,128]{1,0:T(8,128)(2,1)} %shard_map.118) | data formatting | bytes 65536

commit v5 on v4

--- a/solution.py
+++ b/solution.py
@@ -420,22 +420,26 @@
         merge(3, side)
         half_cut = pl.ds(side * near, near)
         go(xo_send.at[2, :, :, half_cut], xo_half.at[side], xo_s.at[side], xo_r.at[side], to)
-    loop(0, 2, lambda i: merge(1 + i, 1 - i))
+    for side, to in ((0, right), (1, left)):
+        merge(1 + side, 1 - side)
+        half_cut = pl.ds((1 - side) * near, near)
+        go(xo_send.at[side, :, :, half_cut], xo_full.at[side, :, :, half_cut], xo_s.at[2 + side], xo_r.at[2 + side], to)
     loop(0, 2, lambda i: merge(0, i))
     for side, to in ((0, right), (1, left)):
         arrived(xo_half.at[side], xo_s.at[side], xo_r.at[side])
         merge(1 + side, side, True)
-        go(xo_send.at[side], xo_full.at[side], xo_s.at[2 + side], xo_r.at[2 + side], to)
+        half_cut = pl.ds(side * near, near)
+        go(xo_send.at[side, :, :, half_cut], xo_full.at[side, :, :, half_cut], xo_s.at[4 + side], xo_r.at[4 + side], to)
     private_o = pr_o[...].T
     private_l = pr_l[...].T[:1]
-    for side in range(2):
-        arrived(xo_full.at[side], xo_s.at[2 + side], xo_r.at[2 + side])
+    for k, side, part_at in ((2, 0, 1), (3, 1, 0), (4, 0, 0), (5, 1, 1)):
+        arrived(xo_full.at[side, :, :, pl.ds(part_at * near, near)], xo_s.at[k], xo_r.at[k])
 
     both = 2 * COLUMNS
     low = iota((D, both), 1) < COLUMNS
 
     def join(i):
-        cut = pl.ds(pl.multiple_of(i * both, both), both)
+        cut = pl.ds(i * both, both)
         halves, marks = [], []
         for kv in range(KV):
             pieces = [(sh_l[0, kv, :1, cut], lambda: sh_o[0, kv, :, cut])]
@@ -454,17 +458,16 @@
         for p, o, lse in ((2 * i, first_o, first_l), (2 * i + 1, second_o, second_l)):
             zo_send[p, :D] = o.astype(BF16)
             zo_send[p, D:] = split3(lse[:1])
-
-        @pl.when(i == 0)
-        def _():
-            zo_own[...] = first_o
-            zl_own[...] = first_l
-
-    loop(0, zcols // both, join, zcols // both)
-    for p in range(1, NZ):
-        q = back(p)
-        to = device(z_of(zorder[p]), x, b, h)
-        go(zo_send.at[p], zo_recv.at[q - 1], zo_s.at[p - 1], zo_r.at[q - 1], to)
+            if p == 0:
+                zo_own[...] = o
+                zl_own[...] = lse
+            else:
+                q = back(p)
+                to = device(z_of(zorder[p]), x, b, h)
+                go(zo_send.at[p], zo_recv.at[q - 1], zo_s.at[p - 1], zo_r.at[q - 1], to)
+
+    for i in reversed(range(zcols // both)):
+        join(i)
 
     arrived(w.at[2, 0], wx_s.at[0], wx_r.at[0])
     go(w.at[2, 0], w.at[3, 0], wx_s.at[2], wx_r.at[2], right)
@@ -557,7 +560,7 @@
         v((NX - 1, zper, 2 * R, D), BF16), v((zper, NX, 2 * R, D), BF16),
         dma((8,)),
     ]
-    for count in (NZ - 1, 9, 5, 4, NZ - 1, NZ - 1, 6, 2 * NH - 1, NX - 1):
+    for count in (NZ - 1, 9, 5, 6, NZ - 1, NZ - 1, 6, 2 * NH - 1, NX - 1):
         scratch += [dma((count,)), dma((count,))]
     hbm = pl.BlockSpec(memory_space=pl.ANY)
     smem = pl.BlockSpec(memory_space=pltpu.SMEM)

time: 94.3 us -> 92.1 us (0.977)
  Pallas kernels: 92.7 us -> 90.5 us
    pallas_call x1, Pallas kernels: 92.7 us -> 90.5 us  [local(): pl.pallas_call(functools.partial(kernel, NZ, NX, NH), out_shape=jax.Shape...]
where the time goes in v5:
time: 92.1 us; the launch traced here: 91.9 us
  Pallas kernels  90.5 us (98%)
  local copies, waits for them, and re-layouts  1.38 us (1%)
    pallas_call x1, Pallas kernels, local(): pl.pallas_call(functools.partial(kernel, NZ, NX, NH), out_shape=jax.Shape...  90.5 us

profile of v5, /device:TPU:1, one launch (start us, length us, event | category | flops | bytes accessed | tf_op | source)
XLA Modules:
  0.0 91.9 jit_solution(348494725039770629)
XLA Ops:
  0.0 90.5 %shard_map.118 = bf16[128,128]{1,0:T(8,128)(2,1)} custom-call(bf16[8,16,128]{2,1,0:T(8,128)(2,1)} %q_hbm.1, bf16[1024,128]{1,0:T(8,128)(2,1)} %bitcast.11, bf16[1024,128]{1,0:T(8,128)(2,1)} %bitcast.12, bf16[8192,128]{1,0:T(8,128)(2,1)} %bitcast.9, bf16[8192,128]{1,0:T(8,128)(2,1)} %bitcast.10, s32[1,512]{1,0:T(1,128)} %bitcast.13, s32[16]{0:T(128)} %tlen_ref.1, ...), custom_call_target="tpu_custom_call" | custom-call | tf_op jit(solution)/shard_map/pallas_call | solution.py:568
  90.5 1.4 %copy.14 = bf16[128,128]{1,0:T(8,128)(2,1)} copy(bf16[128,128]{1,0:T(8,128)(2,1)} %shard_map.118) | data formatting | bytes 65536

commit v6 on v5

--- a/solution.py
+++ b/solution.py
@@ -166,8 +166,8 @@
 
     left, right, far = device(z, x_of(-1), b, h), device(z, x_of(1), b, h), device(z, x_of(2), b, h)
 
-    def z_start(buf, zs, zr):
-        for p in range(1, NZ):
+    def z_start(buf, zs, zr, places):
+        for p in places:
             q = back(p)
             go(buf.at[0, 0], buf.at[0, q], zs.at[p - 1], zr.at[q - 1], device(z_of(zorder[p]), x, b, h))
 
@@ -190,7 +190,7 @@
             k = 3 * group + slot - 1
             arrived(block(slot, group), qx_s.at[k], qx_r.at[k])
 
-    z_start(q_all, qz_s, qz_r)
+    z_start(q_all, qz_s, qz_r, range(1, NZ))
     forward(0)
     loads["sk"].wait()
     go(sk_raw.at[0], sk_raw.at[1], pair_s.at[0], pair_r.at[0], pair)
@@ -324,18 +324,18 @@
     for r in range(R):
         private(r)
     pair_shared()
+
+    def chunk_queries(xx, kv):
+        return q_all[xx, :, kv * COLUMNS:(kv + 1) * COLUMNS, :].reshape(zcols, D)
+
+    found = [dot(onehot[0], chunk_queries(0, kv)) for kv in range(KV)]
     for slot_at in (2, 1, 3):
         x_wait(slot_at)
-
-    def chunk_queries(xx, kv):
-        return q_all[xx, :, kv * COLUMNS:(kv + 1) * COLUMNS, :].reshape(zcols, D)
-
+        found = [
+            sums + dot(onehot[slot_at], chunk_queries(slot_at, kv)) for kv, sums in enumerate(found)
+        ]
     for kv in range(KV):
-        total = dot(onehot[0], chunk_queries(0, kv))
-        for xx in range(1, NX):
-            total += dot(onehot[xx], chunk_queries(xx, kv))
-        qt_send[kv] = total.astype(BF16)
-
+        qt_send[kv] = found[kv].astype(BF16)
     go(qt_send, qt_recv, pair_s.at[3], pair_r.at[3], pair)
 
     go(w.at[0, 0], w.at[2, 0], wx_s.at[0], wx_r.at[0], right)
@@ -343,7 +343,7 @@
     loop(0, 2 * per_slot, shared)
 
     extent = tlen_ref[tenant] - lax.rem(seq, 4) * positions
-    step_size = min(1024, positions)
+    step_size = min(2048, positions)
 
     arrived(w.at[0, 1], pair_s.at[2], pair_r.at[2])
     go(w.at[0, 1], w.at[2, 1], wx_s.at[4], wx_r.at[4], right)
@@ -481,7 +481,7 @@
     attended, _ = combine(pieces)
     at[0, 0] = attended.T.astype(BF16)
 
-    z_start(at, az_s, az_r)
+    z_start(at, az_s, az_r, reversed(range(1, NZ)))
     for group in range(len(groups)):
         z_wait(at, az_s, az_r, group)
     wide = at[0].astype(F32)

time: 92.1 us -> 91.7 us (level)
  no operation moved by 1% of the time
where the time goes in v6:
time: 91.7 us; the launch traced here: 91.6 us
  Pallas kernels  90.2 us (98%)
  local copies, waits for them, and re-layouts  1.38 us (2%)
    pallas_call x1, Pallas kernels, local(): pl.pallas_call(functools.partial(kernel, NZ, NX, NH), out_shape=jax.Shape...  90.2 us

profile of v6, /device:TPU:1, one launch (start us, length us, event | category | flops | bytes accessed | tf_op | source)
XLA Modules:
  0.0 91.6 jit_solution(12629210377806497605)
XLA Ops:
  0.0 90.2 %shard_map.118 = bf16[128,128]{1,0:T(8,128)(2,1)} custom-call(bf16[8,16,128]{2,1,0:T(8,128)(2,1)} %q_hbm.1, bf16[1024,128]{1,0:T(8,128)(2,1)} %bitcast.11, bf16[1024,128]{1,0:T(8,128)(2,1)} %bitcast.12, bf16[8192,128]{1,0:T(8,128)(2,1)} %bitcast.9, bf16[8192,128]{1,0:T(8,128)(2,1)} %bitcast.10, s32[1,512]{1,0:T(1,128)} %bitcast.13, s32[16]{0:T(128)} %tlen_ref.1, ...), custom_call_target="tpu_custom_call" | custom-call | tf_op jit(solution)/shard_map/pallas_call | solution.py:568
  90.2 1.4 %copy.14 = bf16[128,128]{1,0:T(8,128)(2,1)} copy(bf16[128,128]{1,0:T(8,128)(2,1)} %shard_map.118) | data formatting | bytes 65536
